TPU v7x, 256 devices: a whole 4x4x8 slice. The times are simulated.
256 devices in a mesh: pipe: 8 (over z), tensor: 32 (over x, y, core).
Axes of the slice: x: 4, y: 4, z: 8, core: 2. Of those that a mesh axis runs over, the one named last changes fastest.
Arguments:
- fresh_batch: bfloat16 [1024, 6144], P('tensor'), may hold values from -60 to 60
- handed_forward: bfloat16 [8, 1024, 6144], P('pipe', 'tensor'), may hold values from -60 to 60
- saved_inputs: bfloat16 [8, 1024, 6144], P('pipe', 'tensor'), may hold values from -60 to 60
- handed_grads: bfloat16 [8, 1024, 6144], P('pipe', 'tensor'), may hold values from -6 to 6
- loss_grad: bfloat16 [1024, 6144], P('tensor'), may hold values from -6 to 6
- norm_gain: float32 [8, 6144], P('pipe'), may hold values from 0.25 to 1.75
- route_slot: int32 [8, 2, 1024], P('pipe', None, 'tensor'), may hold values from 0 to 8, as said below
- route_weight: float32 [8, 2, 1024], P('pipe', None, 'tensor'), may hold values from 0.25 to 0.95
- w_gate: bfloat16 [8, 6144, 8192], P('pipe', None, 'tensor'), may hold values from -0.078125 to 0.078125
- w_up: bfloat16 [8, 6144, 8192], P('pipe', None, 'tensor'), may hold values from -0.078125 to 0.078125
- w_down: bfloat16 [8, 8192, 6144], P('pipe', 'tensor'), may hold values from -0.0625 to 0.0625
Outputs:
- forward_out: bfloat16 [8, 1024, 6144], P('pipe', 'tensor')
- input_grad: bfloat16 [8, 1024, 6144], P('pipe', 'tensor')
Inputs may be any that keep to these rules, and one draw needn't show every extreme that they name: `route_slot`: for each layer and micro-batch, each aligned block of 32 tokens holds the slots 0 to c - 1 once each, for some c from 4 to 8, and the value 8 (token not routed to the expert) elsewhere; for each layer and micro-batch at least one block has c = 8.
All inputs are finite; a program needn't handle non-finite values.
Results may differ from a plain program's by a relative error of at most 0.007.
Values may be sent and summed in bfloat16 or wider, within the bound.
A program may use at most 128 MiB of HBM per device.

v0:
```python
import jax
import jax.numpy as jnp
from jax import lax
from jax.sharding import PartitionSpec as P

LCAP = 8


EPS = 1e-05


def passed_along(value, axis, by):
    count = lax.axis_size(axis)
    pairs = [(i, i + by) for i in range(count) if 0 <= i + by < count]
    return lax.ppermute(value, axis, pairs)


def normalize(field, gain):
    values = field.astype(jnp.float32)
    inverse = lax.rsqrt(jnp.mean(values * values, axis=-1, keepdims=True) + EPS)
    return (values * inverse * gain, inverse)


def selector(slots, slot_count):
    places = lax.broadcasted_iota(jnp.int32, (slot_count, slots.shape[0]), 0)
    return (places == slots[None, :]).astype(jnp.bfloat16)


def contract_first(left, right):
    return lax.dot_general(
        left, right, (((0,), (0,)), ((), ())), preferred_element_type=jnp.float32
    )


def contract_last(left, right):
    return lax.dot_general(
        left, right, (((1,), (1,)), ((), ())), preferred_element_type=jnp.float32
    )


def on_device(
    fresh_batch,
    handed_forward,
    saved_inputs,
    handed_grads,
    loss_grad,
    norm_gain,
    route_slot,
    route_weight,
    w_gate,
    w_up,
    w_down,
):
    section = lax.axis_index("pipe")
    final_section = lax.axis_size("pipe") - 1
    gain = norm_gain[0]
    gate_weight = w_gate[0]
    up_weight = w_up[0]
    down_weight = w_down[0]
    arrived = passed_along(handed_forward[0], "pipe", 1)
    forward_in = jnp.where(section == 0, fresh_batch, arrived)
    returned = passed_along(handed_grads[0], "pipe", -1)
    grad_in = jnp.where(section == final_section, loss_grad, returned)
    pick_fwd = selector(route_slot[0, 0], LCAP)
    pick_bwd = selector(route_slot[0, 1], LCAP)
    normed_fwd = normalize(forward_in, gain)[0].astype(jnp.bfloat16)
    normed_raw, inverse = normalize(saved_inputs[0], gain)
    normed_bwd = normed_raw.astype(jnp.bfloat16)
    scaled_grad = (route_weight[0, 1][:, None] * grad_in.astype(jnp.float32)).astype(jnp.bfloat16)
    rows_fwd = jnp.dot(pick_fwd, normed_fwd, preferred_element_type=jnp.float32).astype(
        jnp.bfloat16
    )
    rows_bwd = jnp.dot(pick_bwd, normed_bwd, preferred_element_type=jnp.float32).astype(
        jnp.bfloat16
    )
    rows_grad = jnp.dot(pick_bwd, scaled_grad, preferred_element_type=jnp.float32).astype(
        jnp.bfloat16
    )

    def expand(stacked, count_normed):
        with_grad = stacked.shape[1] > count_normed
        piece = lax.all_gather(stacked, "tensor", axis=0, tiled=True)
        results = []
        results.append(jnp.dot(piece[:, 0], gate_weight, preferred_element_type=jnp.float32))
        results.append(jnp.dot(piece[:, 0], up_weight, preferred_element_type=jnp.float32))
        if with_grad:
            results.append(contract_last(piece[:, count_normed], down_weight))
        return jnp.stack(results, axis=1)

    def reduce_rows(producers):
        start = jnp.int32(0)
        return lax.psum_scatter(
            jnp.concatenate(
                [make(start, LCAP * lax.axis_size("tensor")) for make in producers], axis=1
            ).astype(jnp.bfloat16),
            "tensor",
            scatter_dimension=0,
            tiled=True,
        ).astype(jnp.float32)

    def forward_term(hidden):

        def make(start, count):
            return jnp.dot(hidden, down_weight, preferred_element_type=jnp.float32)

        return make

    def backward_term(grad_gate, grad_up):

        def make(start, count):
            return contract_last(grad_gate, gate_weight) + contract_last(grad_up, up_weight)

        return make

    expanded_fwd = expand(rows_fwd[:, None, :], 1)
    hidden = (jax.nn.silu(expanded_fwd[:, 0]) * expanded_fwd[:, 1]).astype(jnp.bfloat16)
    expert_out = reduce_rows([forward_term(hidden)]).astype(jnp.bfloat16)
    expanded_bwd = expand(jnp.stack([rows_bwd, rows_grad], axis=1), 1)
    gate = expanded_bwd[:, 0]
    grad_hidden = expanded_bwd[:, 2]
    sigma = jax.nn.sigmoid(gate)
    grad_gate = (grad_hidden * expanded_bwd[:, 1] * sigma * (1.0 + gate * (1.0 - sigma))).astype(
        jnp.bfloat16
    )
    grad_up = (grad_hidden * jax.nn.silu(gate)).astype(jnp.bfloat16)
    grad_gate, grad_up = (grad_gate, grad_up)
    row_grads = reduce_rows([backward_term(grad_gate, grad_up)]).astype(jnp.bfloat16)
    spread = contract_first(pick_fwd, expert_out)
    forward_out = (forward_in.astype(jnp.float32) + route_weight[0, 0][:, None] * spread).astype(
        jnp.bfloat16
    )
    adjusted = contract_first(pick_bwd, row_grads) * gain
    values = saved_inputs[0].astype(jnp.float32)
    result = (
        grad_in.astype(jnp.float32)
        + adjusted * inverse
        - values
        * (inverse * inverse * inverse)
        * jnp.mean(adjusted * values, axis=-1, keepdims=True)
    )
    return (forward_out[None], result.astype(jnp.bfloat16)[None])


def solution(mesh):
    placed = (
        P("tensor", None),
        P("pipe", "tensor", None),
        P("pipe", "tensor", None),
        P("pipe", "tensor", None),
        P("tensor", None),
        P("pipe", None),
        P("pipe", None, "tensor"),
        P("pipe", None, "tensor"),
        P("pipe", None, "tensor"),
        P("pipe", None, "tensor"),
        P("pipe", "tensor", None),
    )
    return jax.shard_map(
        on_device,
        mesh=mesh,
        in_specs=placed,
        out_specs=(P("pipe", "tensor", None), P("pipe", "tensor", None)),
        check_vma=False,
    )
```

profile of v0, /device:TPU:1, one launch (start us, length us, event | category | flops | bytes accessed | tf_op | source)
XLA Modules:
  0.0 325.6 jit_solution(15151472310344329706)
XLA Ops:
  7.2 0.0 copy-start
  7.2 0.0 copy-start.5
  7.2 0.0 all-gather.6.cloned.1.call-start
  7.2 4.7 %collective-permute-start = (bf16[32,6144]{1,0:T(8,128)(2,1)}, bf16[32,6144]{1,0:T(8,128)(2,1)S(1)}, u32[]{:S(2)}, u32[]{:S(2)}) collective-permute-start(bf16[32,6144]{1,0:T(8,128)(2,1)} %bitcast.87), channel_id=1, source_target_pairs={{0,32},{32,64},{64,96},{96,128},{128,160},{160,192},{192,224},{1,3... | collective-permute-start | bytes 1179656 | tf_op jit(solution)/shard_map/ppermute | solution.py:15
  11.9 0.8 slice_bitcast_fusion.16
  12.7 7.3 %collective-permute-done = bf16[32,6144]{1,0:T(8,128)(2,1)S(1)} collective-permute-done((bf16[32,6144]{1,0:T(8,128)(2,1)}, bf16[32,6144]{1,0:T(8,128)(2,1)S(1)}, u32[]{:S(2)}, u32[]{:S(2)}) %collective-permute-start) | collective-permute-done | bytes 393248 | tf_op jit(solution)/shard_map/ppermute | solution.py:15
  20.0 1.2 fusion.45
  21.2 0.0 copy-start.3
  21.2 0.7 copy-done.3
  22.0 1.6 convolution_convert_fusion.3
  23.6 0.0 all-gather.6.cloned.1.call-update
  23.6 0.0 all-gather.4.cloned.1.call-start
  23.7 1.3 collective-permute-start.1
  25.0 1.2 fusion.48
  26.2 0.6 multiply_multiply_fusion
  26.7 1.3 fusion.4
  28.0 0.0 copy-done.5
  28.0 6.8 %collective-permute-done.1 = bf16[32,6144]{1,0:T(8,128)(2,1)S(1)} collective-permute-done((bf16[32,6144]{1,0:T(8,128)(2,1)}, bf16[32,6144]{1,0:T(8,128)(2,1)S(1)}, u32[]{:S(2)}, u32[]{:S(2)}) %collective-permute-start.1) | collective-permute-done | bytes 393248 | tf_op jit(solution)/shard_map/ppermute | solution.py:15
  34.8 0.0 copy-start.4
  34.8 0.2 fusion.5
  35.1 0.7 pad_maximum_fusion
  35.8 0.0 all-gather.4.cloned.1.call-update
  35.8 0.0 reduce-scatter.3.cloned.1.call-start
  35.9 42.9 %all-gather.6.cloned.1.call-done = bf16[256,6144]{1,0:T(8,128)(2,1)} async-done(((bf16[8,6144]{1,0:T(8,128)(2,1)}), bf16[256,6144]{1,0:T(8,128)(2,1)}) %all-gather.6.cloned.1.call-update) | async-done | bytes 3145744 | tf_op jit(solution)/shard_map/all_gather | solution.py:82
  78.8 4.5 %fusion.18 = f32[256,256]{1,0:T(8,128)} fusion(bf16[256,6144]{1,0:T(8,128)(2,1)} %all-gather.6.cloned.1.call-done, bf16[1,6144,256]{2,1,0:T(8,128)(2,1)} %param.19), kind=kOutput, calls=%fused_computation.27 | convolution fusion | flops 805306368 | bytes 6553600 | tf_op jit(solution)/shard_map/dot_general | solution.py:84
  83.3 0.0 copy-done.4
  83.3 0.0 copy-done
  83.3 8.0 %convolution_convert_fusion = bf16[256,6144]{1,0:T(8,128)(2,1)} fusion(bf16[1,256,6144]{2,1,0:T(8,128)(2,1)} %param.21, bf16[256,6144]{1,0:T(8,128)(2,1)} %all-gather.6.cloned.1.call-done, bf16[1,6144,256]{2,1,0:T(8,128)(2,1)S(1)} %copy-done, f32[256,256]{1,0:T(8,128)} %fusion.18), kind=kOutput, calls=%fused_computation.2 | convolution fusion | flops 1612578816 | bytes 12845056 | tf_op jit(solution)/shard_map/dot_general | solution.py:104
  91.4 0.0 reduce-scatter.3.cloned.1.call-update
  91.4 0.0 reduce-scatter.5.cloned.1.call-start
  91.4 43.6 %all-gather.4.cloned.1.call-done = bf16[256,2,6144]{2,0,1:T(8,128)(2,1)} async-done(((bf16[8,2,6144]{2,0,1:T(8,128)(2,1)}), bf16[256,2,6144]{2,0,1:T(8,128)(2,1)}) %all-gather.4.cloned.1.call-update) | async-done | bytes 6291472 | tf_op jit(solution)/shard_map/all_gather | solution.py:82
  135.0 0.0 copy-start.2
  135.0 4.0 %fusion.16 = f32[256,256]{1,0:T(8,128)S(1)} fusion(bf16[1,6144,256]{2,1,0:T(8,128)(2,1)} %param.19, bf16[256,2,6144]{2,0,1:T(8,128)(2,1)} %all-gather.4.cloned.1.call-done), kind=kOutput, calls=%fused_computation.25 | convolution fusion | flops 805306368 | bytes 6553600 | tf_op jit(solution)/shard_map/dot_general | solution.py:84
  139.0 0.0 copy-done.2
  139.0 3.6 %fusion.6 = f32[256,256]{1,0:T(8,128)} fusion(bf16[256,2,6144]{2,0,1:T(8,128)(2,1)} %all-gather.4.cloned.1.call-done, bf16[1,256,6144]{2,1,0:T(8,128)(2,1)S(1)} %copy-done.2), kind=kOutput, calls=%fused_computation.15 | convolution fusion | flops 805306368 | bytes 6553600 | tf_op jit(solution)/shard_map/dot_general | solution.py:36
  142.6 9.0 %fusion.14 = f32[256,6144]{1,0:T(8,128)} fusion(bf16[1,6144,256]{2,1,0:T(8,128)(2,1)} %param.19, f32[256,256]{1,0:T(8,128)} %fusion.6, bf16[1,6144,256]{2,1,0:T(8,128)(2,1)S(1)} %copy-done, bf16[256,2,6144]{2,0,1:T(8,128)(2,1)} %all-gather.4.cloned.1.call-done, f32[256,256]{1,0:T(8,128)S(1)} %fusion.16), kind=kOutput, calls=%fused_computation.23 | convolution fusion | flops 1611268096 | bytes 16252928 | tf_op jit(solution)/shard_map/dot_general | solution.py:36
  151.6 5.7 %fusion = bf16[256,6144]{1,0:T(8,128)(2,1)} fusion(f32[256,6144]{1,0:T(8,128)} %fusion.14, bf16[1,6144,256]{2,1,0:T(8,128)(2,1)S(1)} %copy-done, f32[256,256]{1,0:T(8,128)} %fusion.6, f32[256,256]{1,0:T(8,128)S(1)} %fusion.16), kind=kOutput, calls=%fused_computation.1 | convolution fusion | flops 808845312 | bytes 13107200 | tf_op jit(solution)/shard_map/dot_general | solution.py:36
  157.3 0.0 copy-start.1
  157.3 0.0 copy-start.6
  157.3 0.0 reduce-scatter.5.cloned.1.call-update
  157.3 66.7 %reduce-scatter.3.cloned.1.call-done = bf16[8,6144]{1,0:T(8,128)(2,1)} async-done(((bf16[256,6144]{1,0:T(8,128)(2,1)}), bf16[8,6144]{1,0:T(8,128)(2,1)}) %reduce-scatter.3.cloned.1.call-update) | async-done | bytes 98320 | tf_op jit(solution)/shard_map/reduce_scatter | solution.py:92
  224.0 2.1 fusion.3
  226.1 89.6 %reduce-scatter.5.cloned.1.call-done = bf16[8,6144]{1,0:T(8,128)(2,1)} async-done(((bf16[256,6144]{1,0:T(8,128)(2,1)}), bf16[8,6144]{1,0:T(8,128)(2,1)}) %reduce-scatter.5.cloned.1.call-update) | async-done | bytes 98320 | tf_op jit(solution)/shard_map/reduce_scatter | solution.py:92
  315.7 0.0 copy-done.1
  315.7 1.3 fusion.52
  317.1 0.0 copy-done.6
  317.1 2.0 fusion.55
  (3 shorter events, 0.0 us)
Async XLA Ops:
  7.2 76.2 %copy-start = (bf16[1,6144,256]{2,1,0:T(8,128)(2,1)S(1)}, bf16[1,6144,256]{2,1,0:T(8,128)(2,1)}, u32[]{:S(2)}) copy-start(bf16[1,6144,256]{2,1,0:T(8,128)(2,1)} %param.20) | copy-start | bytes 9437188
  7.2 20.8 %copy-start.5 = (f32[1,2,32]{2,1,0:T(2,128)S(1)}, f32[1,2,32]{2,1,0:T(2,128)}, u32[]{:S(2)}) copy-start(f32[1,2,32]{2,1,0:T(2,128)} %param.18) | copy-start | bytes 772
  7.2 71.6 %all-gather.6.cloned.1.call-start = ((), (), s32[]{:S(2)}) async-start(), calls=%async_computation.5 | async-start | bytes 3244032 | tf_op jit(solution)/shard_map/all_gather | solution.py:82
  7.2 12.7 %collective-permute-start = (bf16[32,6144]{1,0:T(8,128)(2,1)}, bf16[32,6144]{1,0:T(8,128)(2,1)S(1)}, u32[]{:S(2)}, u32[]{:S(2)}) collective-permute-start(bf16[32,6144]{1,0:T(8,128)(2,1)} %bitcast.87), channel_id=1, source_target_pairs={{0,32},{32,64},{64,96},{96,128},{128,160},{160,192},{192,224},{1,3... | collective-permute-start | bytes 1179656 | tf_op jit(solution)/shard_map/ppermute | solution.py:15
  21.2 0.8 copy-start.3
  23.6 111.4 %all-gather.4.cloned.1.call-start = ((), (), s32[]{:S(2)}) async-start(), calls=%async_computation.3 | async-start | bytes 6488064 | tf_op jit(solution)/shard_map/all_gather | solution.py:82
  23.7 11.2 %collective-permute-start.1 = (bf16[32,6144]{1,0:T(8,128)(2,1)}, bf16[32,6144]{1,0:T(8,128)(2,1)S(1)}, u32[]{:S(2)}, u32[]{:S(2)}) collective-permute-start(bf16[32,6144]{1,0:T(8,128)(2,1)} %bitcast.88), channel_id=1, source_target_pairs={{32,0},{64,32},{96,64},{128,96},{160,128},{192,160},{224,192},{33,... | collective-permute-start | bytes 1179656 | tf_op jit(solution)/shard_map/ppermute | solution.py:15
  34.8 48.5 %copy-start.4 = (bf16[32,6144]{1,0:T(8,128)(2,1)}, bf16[32,6144]{1,0:T(8,128)(2,1)S(1)}, u32[]{:S(2)}) copy-start(bf16[32,6144]{1,0:T(8,128)(2,1)S(1)} %collective-permute-done.1) | copy-start | bytes 1179652
  35.8 188.2 %reduce-scatter.3.cloned.1.call-start = ((), (), s32[]{:S(2)}) async-start(), calls=%async_computation.2 | async-start | bytes 3244032 | tf_op jit(solution)/shard_map/reduce_scatter | solution.py:92
  91.4 224.4 %reduce-scatter.5.cloned.1.call-start = ((), (), s32[]{:S(2)}) async-start(), calls=%async_computation.4 | async-start | bytes 3244032 | tf_op jit(solution)/shard_map/reduce_scatter | solution.py:92
  135.0 4.0 %copy-start.2 = (bf16[1,256,6144]{2,1,0:T(8,128)(2,1)S(1)}, bf16[1,256,6144]{2,1,0:T(8,128)(2,1)}, u32[]{:S(2)}) copy-start(bf16[1,256,6144]{2,1,0:T(8,128)(2,1)} %param.21) | copy-start | bytes 9437188
  157.3 158.5 %copy-start.1 = (bf16[1,32,6144]{2,1,0:T(8,128)(2,1)S(1)}, bf16[1,32,6144]{2,1,0:T(8,128)(2,1)}, u32[]{:S(2)}) copy-start(bf16[1,32,6144]{2,1,0:T(8,128)(2,1)} %param.13) | copy-start | bytes 1179652
  157.3 159.8 %copy-start.6 = (f32[32]{0:T(128)S(1)}, f32[32]{0:T(128)}, u32[]{:S(2)}) copy-start(f32[32]{0:T(128)} %get-tuple-element.8) | copy-start | bytes 388
Sparse Core Ops, SparseCore 0:
  23.7 55.0 all-gather.5
  81.4 53.5 all-gather.3
  138.9 85.0 reduce-scatter.2
  228.3 87.4 reduce-scatter.4
where the time goes:
time: 327 us; the launch traced here: 326 us
  waiting for transfers between devices  257 us (79%)
  matrix products  41.4 us (13%)
  between operations  13.9 us (4%)
  starting transfers between devices  6.11 us (2%)
  other arithmetic  5.7 us (2%)
    reduce_scatter x2, waiting for transfers between devices, reduce_rows(): lax.psum_scatter(jnp.concatenate([make(start, LCAP * lax.axis_size('tenso...  156 us
    all_gather x2, waiting for transfers between devices, expand(): piece = lax.all_gather(stacked, 'tensor', axis=0, tiled=True)  86.5 us
    dot_general x3, matrix products, contract_last(): lax.dot_general(left, right, (((1,), (1,)), ((), ())), preferred_element_...  18.3 us
    ppermute x2, waiting for transfers between devices, passed_along(): return lax.ppermute(value, axis, pairs)  14.1 us
    dot_general x2, matrix products, expand(): jnp.dot(piece[:, 0], gate_weight, preferred_element_type=jnp.float32)  8.48 us
    dot_general x1, matrix products, make(): return jnp.dot(hidden, down_weight, preferred_element_type=jnp.float32)  8.03 us
  transfers between devices with their start and end apart: 6, of which 6 were waited for; matrix products, arithmetic and copies ran while one was open for 13% of the time, Pallas kernels for 0%

commit v1 on v0

v1 whole, which is shorter than its diff:
```python
import functools

import jax
import jax.numpy as jnp
from jax import lax
from jax.experimental import pallas as pl
from jax.experimental.pallas import tpu as pltpu
from jax.sharding import PartitionSpec as P

LCAP = 8
SIDE = 4
PAIR = 2 * LCAP
EPS = 1e-05
F32 = jnp.float32
BF16 = jnp.bfloat16
BWD, GRAD, FWD = 0, 1, 2
ROWG, OUT = 0, 1


def contract_last(left, right):
    return lax.dot_general(left, right, (((1,), (1,)), ((), ())), preferred_element_type=F32)


def kernel(
    n_pipe,
    fresh,
    handed_fwd,
    saved,
    handed_grads,
    loss_grad,
    gain,
    slot,
    weight,
    w_gate,
    w_up,
    w_down,
    out_fwd,
    out_grad,
    saved_v,
    fwd_v,
    grad_v,
    gain_v,
    slot_v,
    weight_v,
    wgu,
    wd,
    picked,
    tile,
    sib_tile,
    rows,
    acc,
    gh,
    act,
    part,
    sib_part,
    b_out,
    b_in,
    w_sum,
    a_out,
    a_in,
    final,
    inverse_v,
    of_v,
    og_v,
    loc_sem,
    z_send,
    z_recv,
    g_send,
    g_recv,
    r_send,
    r_recv,
):
    D = saved.shape[2]
    TOKD = saved.shape[1]
    FFD = w_down.shape[1]
    H = D // 2
    C = D // 4
    LANES = min(1024, H)

    section = lax.axis_index("pipe")
    t = lax.axis_index("tensor")
    core = t % 2
    x = t // (2 * SIDE)
    y = (t // 2) % SIDE
    a = x + core * (y - x)
    b = y + core * (x - y)
    sa = 2 * SIDE - core * (2 * SIDE - 2)
    sb = 2 + core * (2 * SIDE - 2)
    a_up, a_op, a_dn = (a + 1) % SIDE, (a + 2) % SIDE, (a + 3) % SIDE
    b_up, b_op, b_dn = (b + 1) % SIDE, (b + 2) % SIDE, (b + 3) % SIDE
    A_UP = a_up * sa + b * sb + core
    A_DN = a_dn * sa + b * sb + core
    B_UP = a * sa + b_up * sb + core
    B_DN = a * sa + b_dn * sb + core
    SIB = t + 1 - 2 * core
    Z_UP = (section + 1) % n_pipe
    Z_DN = (section + n_pipe - 1) % n_pipe
    own = pl.ds(pl.multiple_of(core * H, H), H)
    oth = pl.ds(pl.multiple_of((1 - core) * H, H), H)

    def at(tensor):
        return {"pipe": section, "tensor": tensor}

    def local(src, dst, k):
        return pltpu.make_async_copy(src, dst, loc_sem.at[k])

    first = [
        local(saved.at[0], saved_v, 0),
        local(gain, gain_v, 1),
        local(slot.at[0], slot_v, 2),
        local(weight.at[0], weight_v, 3),
    ]
    load_gu = [
        local(w_gate.at[0, own], wgu.at[0, :, pl.ds(0, FFD)], 4),
        local(w_gate.at[0, oth], wgu.at[1, :, pl.ds(0, FFD)], 5),
        local(w_up.at[0, own], wgu.at[0, :, pl.ds(FFD, FFD)], 6),
        local(w_up.at[0, oth], wgu.at[1, :, pl.ds(FFD, FFD)], 7),
    ]
    load_d = [
        local(w_down.at[0, :, own], wd.at[0], 8),
        local(w_down.at[0, :, oth], wd.at[1], 9),
    ]
    load_fresh = local(fresh, fwd_v, 10)
    load_loss = local(loss_grad, grad_v, 11)
    store_grad = local(og_v, out_grad.at[0], 12)
    store_fwd = local(of_v, out_fwd.at[0], 13)
    for copy in first:
        copy.start()

    barrier = pltpu.get_barrier_semaphore()
    for tensor in (SIB, A_UP, A_DN, B_UP, B_DN):
        pl.semaphore_signal(
            barrier, inc=1, device_id=at(tensor), device_id_type=pl.DeviceIdType.MESH
        )
    for pipe in (Z_UP, Z_DN):
        pl.semaphore_signal(
            barrier,
            inc=1,
            device_id={"pipe": pipe, "tensor": t},
            device_id_type=pl.DeviceIdType.MESH,
        )
    pl.semaphore_wait(barrier, 7)

    send_fwd = pltpu.make_async_remote_copy(
        src_ref=handed_fwd.at[0],
        dst_ref=fwd_v,
        send_sem=z_send.at[0],
        recv_sem=z_recv.at[0],
        device_id={"pipe": Z_UP, "tensor": t},
        device_id_type=pl.DeviceIdType.MESH,
    )
    send_grad = pltpu.make_async_remote_copy(
        src_ref=handed_grads.at[0],
        dst_ref=grad_v,
        send_sem=z_send.at[1],
        recv_sem=z_recv.at[1],
        device_id={"pipe": Z_DN, "tensor": t},
        device_id_type=pl.DeviceIdType.MESH,
    )

    @pl.when(section != n_pipe - 1)
    def _():
        send_fwd.start()

    @pl.when(section != 0)
    def _():
        send_grad.start()

    @pl.when(section == 0)
    def _():
        load_fresh.start()

    @pl.when(section == n_pipe - 1)
    def _():
        load_loss.start()

    sent = []

    def remote(src, dst, send_sem, recv_sem, tensor):
        copy = pltpu.make_async_remote_copy(
            src_ref=src,
            dst_ref=dst,
            send_sem=send_sem,
            recv_sem=recv_sem,
            device_id=at(tensor),
            device_id_type=pl.DeviceIdType.MESH,
        )
        return copy

    def go(copy):
        copy.start()
        sent.append(copy)
        return copy

    for copy in first:
        copy.wait()

    def row_pick(micro):
        places = lax.broadcasted_iota(jnp.int32, (PAIR, TOKD), 0) - core * LCAP
        slots = jnp.broadcast_to(slot_v[pl.ds(micro, 1), :], (PAIR, TOKD))
        return jnp.where((places == slots) & (places >= 0) & (places < LCAP), 1.0, 0.0)

    def column(row):
        wide = jnp.broadcast_to(row, (TOKD, TOKD))
        eye = lax.broadcasted_iota(jnp.int32, (TOKD, TOKD), 0) == lax.broadcasted_iota(
            jnp.int32, (TOKD, TOKD), 1
        )
        return jnp.sum(jnp.where(eye, wide, 0.0), axis=1, keepdims=True)

    def token_pick(micro):
        slots = column(slot_v[pl.ds(micro, 1), :].astype(F32))
        slots = jnp.broadcast_to(slots, (TOKD, PAIR))
        places = (
            lax.broadcasted_iota(jnp.int32, (TOKD, PAIR), 1) - core * LCAP
        ).astype(F32)
        return jnp.where(
            (places == slots) & (places >= 0.0) & (places < float(LCAP)), 1.0, 0.0
        ).astype(BF16)

    def lanes(k):
        return pl.ds(pl.multiple_of(k * LANES, LANES), LANES)

    def normed_tile(i, source, micro):
        pick = row_pick(micro).astype(BF16)

        def square(k, total):
            z = jnp.dot(pick, source[:, lanes(k)], preferred_element_type=F32)
            picked[:, lanes(k)] = z
            return total + jnp.sum(z * z, axis=1, keepdims=True)

        total = lax.fori_loop(0, D // LANES, square, jnp.zeros((PAIR, 1), F32))
        inverse = lax.rsqrt(total * (1.0 / D) + EPS)

        def scale(k, carry):
            tile[i, :, lanes(k)] = (
                picked[:, lanes(k)] * inverse * gain_v[:, lanes(k)]
            ).astype(BF16)
            return carry

        lax.fori_loop(0, D // LANES, scale, 0)

    def grad_tile(i, source, micro):
        pick_f = row_pick(micro)
        pick = pick_f.astype(BF16)
        weights = jnp.sum(
            pick_f * jnp.broadcast_to(weight_v[pl.ds(micro, 1), :], (PAIR, TOKD)),
            axis=1,
            keepdims=True,
        )

        def scale(k, carry):
            g = jnp.dot(pick, source[:, lanes(k)], preferred_element_type=F32)
            tile[i, :, lanes(k)] = (weights * g).astype(BF16)
            return carry

        lax.fori_loop(0, D // LANES, scale, 0)

    C0, C1 = pl.ds(0, C), pl.ds(C, C)

    def gather(i):
        def sems(m):
            return g_send.at[i, m], g_recv.at[i, m]

        mine = rows.at[i, 0]
        copies = {
            "tile": remote(tile.at[i, :, oth], sib_tile.at[i], *sems(0), SIB),
            "a_up": remote(mine.at[b, a], mine.at[b, a], *sems(1), A_UP),
            "a_dn": remote(mine.at[b, a], mine.at[b, a], *sems(2), A_DN),
            "a_up2": remote(
                mine.at[b, a_dn, :, C0], mine.at[b, a_dn, :, C0], *sems(3), A_UP
            ),
            "a_dn2": remote(
                mine.at[b, a_up, :, C1], mine.at[b, a_up, :, C1], *sems(4), A_DN
            ),
            "b_up": remote(mine.at[b], mine.at[b], *sems(5), B_UP),
            "b_dn": remote(mine.at[b], mine.at[b], *sems(6), B_DN),
            "b_up2": remote(
                mine.at[b_dn, :, :, C0], mine.at[b_dn, :, :, C0], *sems(7), B_UP
            ),
            "b_dn2": remote(
                mine.at[b_up, :, :, C1], mine.at[b_up, :, :, C1], *sems(8), B_DN
            ),
        }
        for m, line in enumerate((b, b_dn, b_up, b_op)):
            copies["s", m] = remote(
                mine.at[line], rows.at[i, 1, :, line], *sems(9 + m), SIB
            )
        return copies

    g = [gather(i) for i in range(3)]

    def e0(i):
        go(g[i]["tile"])

    def e1(i):
        g[i]["tile"].wait_recv()
        rows[i, 0, b, a] = tile[i, :, own] + sib_tile[i]
        go(g[i]["a_up"])
        go(g[i]["a_dn"])

    def e2(i):
        g[i]["a_up"].wait_recv()
        go(g[i]["a_up2"])
        g[i]["a_dn"].wait_recv()
        go(g[i]["a_dn2"])

    def e3(i):
        g[i]["a_up2"].wait_recv()
        g[i]["a_dn2"].wait_recv()
        go(g[i]["b_up"])
        go(g[i]["b_dn"])
        go(g[i]["s", 0])

    def e4(i):
        g[i]["b_up"].wait_recv()
        go(g[i]["b_up2"])
        go(g[i]["s", 1])
        g[i]["b_dn"].wait_recv()
        go(g[i]["b_dn2"])
        go(g[i]["s", 2])

    def e5(i):
        g[i]["b_up2"].wait_recv()
        g[i]["b_dn2"].wait_recv()
        go(g[i]["s", 3])

    def e6(i):
        for m in range(4):
            g[i]["s", m].wait_recv()

    FLAT = SIDE * SIDE * PAIR
    KC = C

    def gate_up(i):
        for h in range(2):
            for c in range(2):
                cols = pl.ds(c * KC, KC)
                term = jnp.dot(
                    rows[i, h, :, :, :, cols].reshape(FLAT, KC),
                    wgu[h, cols, :],
                    preferred_element_type=F32,
                )
                acc[...] = term if (h, c) == (0, 0) else acc[...] + term

    def grad_hidden():
        for h in range(2):
            for c in range(2):
                cols = pl.ds(c * KC, KC)
                term = contract_last(
                    rows[GRAD, h, :, :, :, cols].reshape(FLAT, KC), wd[h, :, cols]
                )
                gh[...] = term if (h, c) == (0, 0) else gh[...] + term

    def silu(v):
        return v * jax.nn.sigmoid(v)

    NC = C // 3 if C % 384 == 0 else C

    def partial(j, h, c):
        for n in range(C // NC):
            if j == OUT:
                term = jnp.dot(
                    act[:, pl.ds(0, FFD)],
                    wd[h, :, pl.ds(c * C + n * NC, NC)],
                    preferred_element_type=F32,
                )
            else:
                term = contract_last(act[...], wgu[h, pl.ds(c * C + n * NC, NC), :])
            part[j, h, c, :, :, :, pl.ds(n * NC, NC)] = term.astype(BF16).reshape(
                SIDE, SIDE, PAIR, NC
            )

    def reduction(j):
        def sems(m):
            return r_send.at[j, m], r_recv.at[j, m]

        copies = {}
        for c in range(2):
            copies["sib", c] = remote(part.at[j, 1, c], sib_part.at[j, c], *sems(c), SIB)
        for m, tensor in enumerate((B_UP, B_DN, B_DN, B_UP, B_UP, B_DN)):
            copies["b", m] = remote(b_out.at[j, m], b_in.at[j, m], *sems(2 + m), tensor)
        for m, tensor in enumerate((A_UP, A_DN, A_DN, A_UP, A_UP, A_DN)):
            copies["a", m] = remote(a_out.at[j, m], a_in.at[j, m], *sems(8 + m), tensor)
        copies["end"] = remote(final.at[j, :, own], final.at[j, :, own], *sems(14), SIB)
        return copies

    r = [reduction(j) for j in range(2)]

    def chip_sum(j, line, c, place):
        return part[j, 0, c, line, place].astype(F32) + sib_part[j, c, place, line].astype(F32)

    def send_b(j, m, line, c, plus=None):
        for place in range(SIDE):
            value = chip_sum(j, line, c, place)
            if plus is not None:
                value = value + b_in[j, plus, place].astype(F32)
            b_out[j, m, place] = value.astype(BF16)
        go(r[j]["b", m])

    def s1(j, c):
        go(r[j]["sib", c])

    def s2(j):
        r[j]["sib", 0].wait_recv()
        send_b(j, 0, b_op, 0)
        r[j]["sib", 1].wait_recv()
        send_b(j, 1, b_op, 1)
        send_b(j, 2, b_dn, 0)
        send_b(j, 3, b_up, 1)

    def s4(j):
        r[j]["b", 0].wait_recv()
        send_b(j, 4, b_up, 0, plus=0)
        r[j]["b", 1].wait_recv()
        send_b(j, 5, b_dn, 1, plus=1)

    def send_a(j, m, place, c, plus=None):
        value = w_sum[j, c, place]
        if plus is not None:
            value = value + a_in[j, plus].astype(F32)
        a_out[j, m] = value.astype(BF16)
        go(r[j]["a", m])

    def s5(j):
        for c, (one, two) in enumerate(((2, 4), (3, 5))):
            r[j]["b", one].wait_recv()
            r[j]["b", two].wait_recv()
            for place in range(SIDE):
                w_sum[j, c, place] = (
                    chip_sum(j, b, c, place)
                    + b_in[j, one, place].astype(F32)
                    + b_in[j, two, place].astype(F32)
                )
            if c == 0:
                send_a(j, 0, a_op, 0)
                send_a(j, 2, a_dn, 0)
            else:
                send_a(j, 1, a_op, 1)
                send_a(j, 3, a_up, 1)

    def s7(j):
        r[j]["a", 0].wait_recv()
        send_a(j, 4, a_up, 0, plus=0)
        r[j]["a", 1].wait_recv()
        send_a(j, 5, a_dn, 1, plus=1)

    def s8(j):
        for c, (one, two) in enumerate(((2, 4), (3, 5))):
            r[j]["a", one].wait_recv()
            r[j]["a", two].wait_recv()
            value = (
                w_sum[j, c, a] + a_in[j, one].astype(F32) + a_in[j, two].astype(F32)
            )
            final[j, :, pl.ds(pl.multiple_of(core * H + c * C, C), C)] = value.astype(BF16)
        go(r[j]["end"])

    normed_tile(BWD, saved_v, 1)
    e0(BWD)
    for copy in load_gu + load_d:
        copy.start()
    e1(BWD)

    def inverse_of(k, total):
        z = saved_v[:, lanes(k)].astype(F32)
        return total + jnp.sum(z * z, axis=1, keepdims=True)

    total = lax.fori_loop(0, D // LANES, inverse_of, jnp.zeros((TOKD, 1), F32))
    inverse_v[...] = jnp.broadcast_to(lax.rsqrt(total * (1.0 / D) + EPS), inverse_v.shape)
    e2(BWD)
    e3(BWD)

    @pl.when(section != n_pipe - 1)
    def _():
        send_grad.wait_recv()

    @pl.when(section == n_pipe - 1)
    def _():
        load_loss.wait()

    grad_tile(GRAD, grad_v, 1)
    e0(GRAD)
    e4(BWD)
    e1(GRAD)

    @pl.when(section != 0)
    def _():
        send_fwd.wait_recv()

    @pl.when(section == 0)
    def _():
        load_fresh.wait()

    normed_tile(FWD, fwd_v, 0)
    e0(FWD)
    e2(GRAD)
    e5(BWD)
    e3(GRAD)
    e1(FWD)
    e6(BWD)
    for copy in load_gu:
        copy.wait()
    gate_up(BWD)
    e2(FWD)
    e4(GRAD)
    e3(FWD)
    e5(GRAD)
    e6(GRAD)
    for copy in load_d:
        copy.wait()
    grad_hidden()
    gate = acc[:, pl.ds(0, FFD)]
    sigma = jax.nn.sigmoid(gate)
    act[:, pl.ds(0, FFD)] = (
        gh[...] * acc[:, pl.ds(FFD, FFD)] * sigma * (1.0 + gate * (1.0 - sigma))
    ).astype(BF16)
    act[:, pl.ds(FFD, FFD)] = (gh[...] * (gate * sigma)).astype(BF16)
    partial(ROWG, 1, 0)
    s1(ROWG, 0)
    partial(ROWG, 1, 1)
    s1(ROWG, 1)
    e4(FWD)
    partial(ROWG, 0, 0)
    partial(ROWG, 0, 1)
    e5(FWD)
    s2(ROWG)
    e6(FWD)
    gate_up(FWD)
    act[:, pl.ds(0, FFD)] = (silu(acc[:, pl.ds(0, FFD)]) * acc[:, pl.ds(FFD, FFD)]).astype(BF16)
    s4(ROWG)
    partial(OUT, 1, 0)
    s1(OUT, 0)
    partial(OUT, 1, 1)
    s1(OUT, 1)
    partial(OUT, 0, 0)
    partial(OUT, 0, 1)
    s2(OUT)
    s5(ROWG)
    s4(OUT)
    s7(ROWG)
    s8(ROWG)
    s5(OUT)

    r[ROWG]["end"].wait_recv()
    pick_bwd = token_pick(1)

    def project(k, total):
        adjusted = (
            jnp.dot(pick_bwd, final[ROWG, :, lanes(k)], preferred_element_type=F32)
            * gain_v[:, lanes(k)]
        )
        return total + jnp.sum(
            adjusted * saved_v[:, lanes(k)].astype(F32), axis=1, keepdims=True
        )

    total = lax.fori_loop(0, D // LANES, project, jnp.zeros((TOKD, 1), F32))
    inverse = inverse_v[:, pl.ds(0, 1)]
    factor = (inverse * inverse * inverse) * (total * (1.0 / D))

    def finish_grad(k, carry):
        adjusted = (
            jnp.dot(pick_bwd, final[ROWG, :, lanes(k)], preferred_element_type=F32)
            * gain_v[:, lanes(k)]
        )
        og_v[:, lanes(k)] = (
            grad_v[:, lanes(k)].astype(F32)
            + adjusted * inverse
            - saved_v[:, lanes(k)].astype(F32) * factor
        ).astype(BF16)
        return carry

    s7(OUT)
    lax.fori_loop(0, D // LANES, finish_grad, 0)
    store_grad.start()

    s8(OUT)
    pick_fwd = token_pick(0)
    scale = column(weight_v[pl.ds(0, 1), :])
    r[OUT]["end"].wait_recv()

    def finish_fwd(k, carry):
        spread = jnp.dot(pick_fwd, final[OUT, :, lanes(k)], preferred_element_type=F32)
        of_v[:, lanes(k)] = (fwd_v[:, lanes(k)].astype(F32) + scale * spread).astype(BF16)
        return carry

    lax.fori_loop(0, D // LANES, finish_fwd, 0)
    store_fwd.start()
    for copy in sent:
        copy.wait_send()

    @pl.when(section != n_pipe - 1)
    def _():
        send_fwd.wait_send()

    @pl.when(section != 0)
    def _():
        send_grad.wait_send()

    store_grad.wait()
    store_fwd.wait()


def on_device(
    n_pipe,
    fresh_batch,
    handed_forward,
    saved_inputs,
    handed_grads,
    loss_grad,
    norm_gain,
    route_slot,
    route_weight,
    w_gate,
    w_up,
    w_down,
):
    TOKD, D = fresh_batch.shape
    FFD = w_down.shape[1]
    H, C = D // 2, D // 4
    FLAT = SIDE * SIDE * PAIR
    anywhere = pl.BlockSpec(memory_space=pl.ANY)
    vmem = pltpu.VMEM
    dma = pltpu.SemaphoreType.DMA
    shape = jax.ShapeDtypeStruct((1, TOKD, D), BF16)
    return pl.pallas_call(
        functools.partial(kernel, n_pipe),
        out_shape=(shape, shape),
        in_specs=[anywhere] * 11,
        out_specs=(anywhere, anywhere),
        scratch_shapes=[
            vmem((TOKD, D), BF16),
            vmem((TOKD, D), BF16),
            vmem((TOKD, D), BF16),
            vmem((1, D), F32),
            vmem((2, TOKD), jnp.int32),
            vmem((2, TOKD), F32),
            vmem((2, H, 2 * FFD), BF16),
            vmem((2, FFD, H), BF16),
            vmem((PAIR, D), F32),
            vmem((3, PAIR, D), BF16),
            vmem((3, PAIR, H), BF16),
            vmem((3, 2, SIDE, SIDE, PAIR, H), BF16),
            vmem((FLAT, 2 * FFD), F32),
            vmem((FLAT, FFD), F32),
            vmem((FLAT, 2 * FFD), BF16),
            vmem((2, 2, 2, SIDE, SIDE, PAIR, C), BF16),
            vmem((2, 2, SIDE, SIDE, PAIR, C), BF16),
            vmem((2, 6, SIDE, PAIR, C), BF16),
            vmem((2, 6, SIDE, PAIR, C), BF16),
            vmem((2, 2, SIDE, PAIR, C), F32),
            vmem((2, 6, PAIR, C), BF16),
            vmem((2, 6, PAIR, C), BF16),
            vmem((2, PAIR, D), BF16),
            vmem((TOKD, 128), F32),
            vmem((TOKD, D), BF16),
            vmem((TOKD, D), BF16),
            dma((14,)),
            dma((2,)),
            dma((2,)),
            dma((3, 13)),
            dma((3, 13)),
            dma((2, 15)),
            dma((2, 15)),
        ],
        compiler_params=pltpu.CompilerParams(
            collective_id=0, has_side_effects=True, vmem_limit_bytes=56 * 2**20
        ),
    )(
        fresh_batch,
        handed_forward,
        saved_inputs,
        handed_grads,
        loss_grad,
        norm_gain,
        route_slot,
        route_weight,
        w_gate,
        w_up,
        w_down,
    )


def solution(mesh):
    placed = (
        P("tensor", None),
        P("pipe", "tensor", None),
        P("pipe", "tensor", None),
        P("pipe", "tensor", None),
        P("tensor", None),
        P("pipe", None),
        P("pipe", None, "tensor"),
        P("pipe", None, "tensor"),
        P("pipe", None, "tensor"),
        P("pipe", None, "tensor"),
        P("pipe", "tensor", None),
    )
    return jax.shard_map(
        functools.partial(on_device, mesh.shape["pipe"]),
        mesh=mesh,
        in_specs=placed,
        out_specs=(P("pipe", "tensor", None), P("pipe", "tensor", None)),
        check_vma=False,
    )
```

time: 327 us -> 90.6 us (0.28)
  waiting for transfers between devices: 257 us -> 0 us
  Pallas kernels: 0 us -> 86.3 us
  matrix products: 41.4 us -> 0 us
  between operations: 13.9 us -> 0.64 us
  starting transfers between devices: 6.11 us -> 0 us
  other arithmetic: 5.7 us -> 0 us
    reduce_scatter x2 -> x0, waiting for transfers between devices: 156 us -> none  [reduce_rows(): lax.psum_scatter(jnp.concatenate([make(start, LCAP * lax.axis_size('tenso...]
    all_gather x2 -> x0, waiting for transfers between devices: 86.5 us -> none  [expand(): piece = lax.all_gather(stacked, 'tensor', axis=0, tiled=True)]
    pallas_call x0 -> x1, Pallas kernels: none -> 86.3 us  [on_device(): pl.pallas_call(functools.partial(kernel, n_pipe), out_shape=(shape, shape...]
    dot_general x11 -> x0, matrix products: 41.4 us -> none  [the longest x3 18.3 us: contract_last(): lax.dot_general(left, right, (((1,), (1,)), ((), ())), preferred_element_...]
    ppermute x2 -> x0, waiting for transfers between devices: 14.1 us -> none  [passed_along(): return lax.ppermute(value, axis, pairs)]
    ppermute x2 -> x0, starting transfers between devices: 5.95 us -> none  [passed_along(): return lax.ppermute(value, axis, pairs)]
  transfers between devices with their start and end apart: 6 -> 0, of which waited for: 6 -> 0; matrix products, arithmetic and copies ran while one was open for 13% -> 0% of each run, Pallas kernels for 0% -> 0%
where the time goes in v1:
time: 90.6 us; the launch traced here: 90.5 us
  Pallas kernels  86.3 us (95%)
  local copies, waits for them, and re-layouts  3.53 us (4%)
    pallas_call x1, Pallas kernels, on_device(): pl.pallas_call(functools.partial(kernel, n_pipe), out_shape=(shape, shape...  86.3 us
    unnamed x2, local copies, waits for them, and re-layouts  3.53 us

profile of v1, /device:TPU:1, one launch (start us, length us, event | category | flops | bytes accessed | tf_op | source)
XLA Modules:
  0.0 90.5 jit_solution(13384580140637468079)
XLA Ops:
  0.6 86.3 %shard_map.122 = (bf16[1,32,6144]{2,1,0:T(8,128)(2,1)}, bf16[1,32,6144]{2,1,0:T(8,128)(2,1)}) custom-call(bf16[32,6144]{1,0:T(8,128)(2,1)} %fresh.1, bf16[1,32,6144]{2,1,0:T(8,128)(2,1)} %handed_fwd.1, bf16[1,32,6144]{2,1,0:T(8,128)(2,1)} %saved.1, bf16[1,32,6144]{2,1,0:T(8,128)(2,1)} %handed_grads.1, bf16[32,6144]{1,0:T(8,128)(2,1)} %loss_grad.1, ...), custom_call_target="tpu_custom_call" | custom-call | tf_op jit(solution)/shard_map/pallas_call | solution.py:624
  86.9 1.8 %copy.15 = bf16[1,32,6144]{2,1,0:T(8,128)(2,1)} copy(bf16[1,32,6144]{2,1,0:T(8,128)(2,1)} %get-tuple-element.4) | data formatting | bytes 786432
  88.7 1.8 %copy.16 = bf16[1,32,6144]{2,1,0:T(8,128)(2,1)} copy(bf16[1,32,6144]{2,1,0:T(8,128)(2,1)} %get-tuple-element.5) | data formatting | bytes 786432

commit v2 on v0

v2 whole, which is shorter than its diff:
```python
import functools

import jax
import jax.numpy as jnp
from jax import lax
from jax.experimental import pallas as pl
from jax.experimental.pallas import tpu as pltpu
from jax.sharding import PartitionSpec as P

LCAP = 8
SIDE = 4
PAIR = 2 * LCAP
EPS = 1e-05
F32 = jnp.float32
BF16 = jnp.bfloat16
BWD, GRAD, FWD = 0, 1, 2
ROWG, OUT = 0, 1


def contract_last(left, right):
    return lax.dot_general(left, right, (((1,), (1,)), ((), ())), preferred_element_type=F32)
ORDER = (
    ("own", 0), ("weights_gu",), ("own_b", 0), ("pair", 0), ("fd", 0, 0), ("opposite", 0),
    ("fu", 0, 1), ("tile", 1), ("fd", 0, 1), ("fu", 0, 0), ("fd", 0, 2), ("own", 1),
    ("fu", 0, 2), ("tile", 2), ("own_b", 1), ("last_pair", 0), ("own", 2), ("last", 0),
    ("pair", 1), ("opposite", 1), ("gu", 0, 0), ("fd", 1, 0), ("fu", 1, 0), ("weights_d",),
    ("own_b", 2), ("fd", 1, 1), ("fu", 1, 1), ("fd", 1, 2), ("fu", 1, 2), ("pair", 2),
    ("handed", 0), ("opposite", 2), ("fu", 2, 0), ("fd", 2, 0), ("gu", 0, 1), ("last_pair", 1),
    ("last", 1), ("gh", 0), ("handed", 1), ("gh", 1), ("act_rowg",), ("fu", 2, 1), ("fd", 2, 1),
    ("p0", 0, 0), ("fd", 2, 2), ("fu", 2, 2), ("p1", 0, 1), ("p1", 0, 0), ("p0", 0, 1),
    ("m1", 0), ("last_pair", 2), ("m3", 0), ("last", 2), ("gu", 2, 0), ("m0", 0), ("m2", 0),
    ("handed", 2), ("gu", 2, 1), ("act_out",), ("p1", 1, 0), ("p1", 1, 1), ("p0", 1, 0),
    ("m0", 1), ("m5", 0), ("p0", 1, 1), ("m3", 1), ("m1", 1), ("m2", 1), ("m4", 0), ("m4", 1),
    ("m5", 1), ("w", 0, 0), ("w", 0, 1), ("w", 1, 0), ("w", 1, 1), ("x", 0, 0), ("x", 0, 1),
    ("x", 1, 0), ("ended", 0), ("project",), ("x", 1, 1), ("finish_fwd", 0), ("finish_grad",),
    ("ended", 1), ("finish_fwd", 1),
)


def kernel(
    n_pipe,
    fresh,
    handed_fwd,
    saved,
    handed_grads,
    loss_grad,
    gain,
    slot,
    weight,
    w_gate,
    w_up,
    w_down,
    out_fwd,
    out_grad,
    saved_v,
    fwd_v,
    grad_v,
    gain_v,
    slot_v,
    weight_v,
    wgu,
    wd,
    picked,
    tile,
    sib_tile,
    rows,
    acc,
    gh,
    act,
    part,
    sib_part,
    b_out,
    b_in,
    w_sum,
    a_out,
    a_in,
    final,
    inverse_v,
    changes,
    loc_sem,
    z_send,
    z_recv,
    g_send,
    g_recv,
    r_send,
    r_recv,
):
    D = saved.shape[2]
    TOKD = saved.shape[1]
    FFD = w_down.shape[1]
    H = D // 2
    C = D // 4
    LANES = min(1024, H)

    section = lax.axis_index("pipe")
    t = lax.axis_index("tensor")
    core = t % 2
    x = t // (2 * SIDE)
    y = (t // 2) % SIDE
    a = x + core * (y - x)
    b = y + core * (x - y)
    sa = 2 * SIDE - core * (2 * SIDE - 2)
    sb = 2 + core * (2 * SIDE - 2)
    A_UP = ((a + 1) % SIDE) * sa + b * sb + core
    A_OP = ((a + 2) % SIDE) * sa + b * sb + core
    A_DN = ((a + 3) % SIDE) * sa + b * sb + core
    B_UP = a * sa + ((b + 1) % SIDE) * sb + core
    B_DN = a * sa + ((b + 3) % SIDE) * sb + core
    SIB = t + 1 - 2 * core
    Z_UP = (section + 1) % n_pipe
    Z_DN = (section + n_pipe - 1) % n_pipe
    own_cols = pl.ds(pl.multiple_of(core * H, H), H)
    oth = pl.ds(pl.multiple_of((1 - core) * H, H), H)

    def at(tensor):
        return {"pipe": section, "tensor": tensor}

    def local(src, dst, k):
        return pltpu.make_async_copy(src, dst, loc_sem.at[k])

    first = [
        local(saved.at[0], saved_v, 0),
        local(gain, gain_v, 1),
        local(slot.at[0], slot_v, 2),
        local(weight.at[0], weight_v, 3),
    ]
    load_gu = [
        local(w_gate.at[0, own_cols], wgu.at[0, :, pl.ds(0, FFD)], 4),
        local(w_gate.at[0, oth], wgu.at[1, :, pl.ds(0, FFD)], 5),
        local(w_up.at[0, own_cols], wgu.at[0, :, pl.ds(FFD, FFD)], 6),
        local(w_up.at[0, oth], wgu.at[1, :, pl.ds(FFD, FFD)], 7),
    ]
    load_d = [
        local(w_down.at[0, :, own_cols], wd.at[0], 8),
        local(w_down.at[0, :, oth], wd.at[1], 9),
    ]
    load_fresh = local(fresh, fwd_v, 10)
    load_loss = local(loss_grad, grad_v, 11)
    for copy in first:
        copy.start()

    barrier = pltpu.get_barrier_semaphore()
    for tensor in (SIB, A_UP, A_OP, A_DN, B_UP, B_DN):
        pl.semaphore_signal(
            barrier, inc=1, device_id=at(tensor), device_id_type=pl.DeviceIdType.MESH
        )
    for pipe in (Z_UP, Z_DN):
        pl.semaphore_signal(
            barrier,
            inc=1,
            device_id={"pipe": pipe, "tensor": t},
            device_id_type=pl.DeviceIdType.MESH,
        )
    sent = []

    def remote(src, dst, send_sem, recv_sem, tensor):
        copy = pltpu.make_async_remote_copy(
            src_ref=src,
            dst_ref=dst,
            send_sem=send_sem,
            recv_sem=recv_sem,
            device_id=at(tensor),
            device_id_type=pl.DeviceIdType.MESH,
        )
        return copy

    def go(copy):
        copy.start()
        sent.append(copy)
        return copy

    for copy in first:
        copy.wait()

    def row_pick(micro):
        places = lax.broadcasted_iota(jnp.int32, (PAIR, TOKD), 0) - core * LCAP
        slots = jnp.broadcast_to(slot_v[pl.ds(micro, 1), :], (PAIR, TOKD))
        return jnp.where((places == slots) & (places >= 0) & (places < LCAP), 1.0, 0.0)

    def column(row):
        wide = jnp.broadcast_to(row, (TOKD, TOKD))
        eye = lax.broadcasted_iota(jnp.int32, (TOKD, TOKD), 0) == lax.broadcasted_iota(
            jnp.int32, (TOKD, TOKD), 1
        )
        return jnp.sum(jnp.where(eye, wide, 0.0), axis=1, keepdims=True)

    def token_pick(micro):
        slots = column(slot_v[pl.ds(micro, 1), :].astype(F32))
        slots = jnp.broadcast_to(slots, (TOKD, PAIR))
        places = (
            lax.broadcasted_iota(jnp.int32, (TOKD, PAIR), 1) - core * LCAP
        ).astype(F32)
        return jnp.where(
            (places == slots) & (places >= 0.0) & (places < float(LCAP)), 1.0, 0.0
        ).astype(BF16)

    def lanes(k):
        return pl.ds(k * LANES, LANES)

    def normed_tile(i, source, micro):
        pick = row_pick(micro).astype(BF16)
        place = 0 if i == BWD else 1
        total = jnp.zeros((PAIR, 1), F32)
        for k in range(D // LANES):
            z = jnp.dot(pick, source[:, lanes(k)], preferred_element_type=F32)
            picked[place, :, lanes(k)] = z
            total = total + jnp.sum(z * z, axis=1, keepdims=True)
        inverse = lax.rsqrt(total * (1.0 / D) + EPS)
        for k in range(D // LANES):
            tile[i, :, lanes(k)] = (
                picked[place, :, lanes(k)] * inverse * gain_v[:, lanes(k)]
            ).astype(BF16)
        return inverse

    def grad_tile(i, source, micro):
        pick_f = row_pick(micro)
        pick = pick_f.astype(BF16)
        weights = jnp.sum(
            pick_f * jnp.broadcast_to(weight_v[pl.ds(micro, 1), :], (PAIR, TOKD)),
            axis=1,
            keepdims=True,
        )

        for k in range(D // LANES):
            g = jnp.dot(pick, source[:, lanes(k)], preferred_element_type=F32)
            tile[i, :, lanes(k)] = (weights * g).astype(BF16)

    C0, C1 = pl.ds(0, C), pl.ds(C, C)
    PAIR_OF = pl.ds(1, 2)

    def gather(i):
        count = iter(range(21))

        def send(src, dst, tensor):
            m = next(count)
            return remote(src, dst, g_send.at[i, m], g_recv.at[i, m], tensor)

        mine = rows.at[i, 0]
        copies = {
            "tile": send(tile.at[i, :, oth], sib_tile.at[i], SIB),
            "au": send(mine.at[0, 0], mine.at[0, 2], A_UP),
            "ad": send(mine.at[0, 0], mine.at[0, 1], A_DN),
            "ax": send(mine.at[0, 0], mine.at[0, 3], A_OP),
        }
        for k, group in enumerate((pl.ds(0, 1), PAIR_OF, pl.ds(3, 1))):
            copies["bu", k] = send(mine.at[0, group], mine.at[2, group], B_UP)
            copies["bd", k] = send(mine.at[0, group], mine.at[1, group], B_DN)
            copies["bu2", k] = send(
                mine.at[2, group, :, C0], mine.at[3, group, :, C0], B_UP
            )
            copies["bd2", k] = send(
                mine.at[1, group, :, C1], mine.at[3, group, :, C1], B_DN
            )
        for line in range(3):
            copies["s", line] = send(mine.at[line], rows.at[i, 1, :, line], SIB)
        first = pl.ds(0, 3)
        copies["s", 3] = send(mine.at[3, first], rows.at[i, 1, first, 3], SIB)
        copies["s", 4] = send(mine.at[3, 3], rows.at[i, 1, 3, 3], SIB)
        return copies

    g = [gather(i) for i in range(3)]

    def reduction(j):
        count = iter(range(20))

        def send(src, dst, tensor):
            m = next(count)
            return remote(src, dst, r_send.at[j, m], r_recv.at[j, m], tensor)

        copies = {}
        for k, lines in enumerate((pl.ds(3, 1), PAIR_OF, pl.ds(0, 1))):
            for c in range(2):
                copies["sib", k, c] = send(
                    part.at[j, 1, c, lines], sib_part.at[j, c, lines], SIB
                )
        for m, tensor in enumerate((B_UP, B_DN, B_DN, B_UP, B_UP, B_DN)):
            copies["b", m] = send(b_out.at[j, m], b_in.at[j, m], tensor)
        for c in range(2):
            for m, tensor in enumerate((A_UP, A_DN, A_OP)):
                copies["a", c, m] = send(a_out.at[j, c, m], a_in.at[j, c, m], tensor)
            cols = pl.ds(pl.multiple_of(core * H + c * C, C), C)
            copies["end", c] = send(final.at[j, :, cols], final.at[j, :, cols], SIB)
        return copies

    r = [reduction(j) for j in range(2)]

    def arrive(copy):
        copy.wait_recv()

    KC = C
    FLAT = SIDE * SIDE * PAIR

    def accumulate(dst, i, h, product):
        for c in range(2):
            cols = pl.ds(c * KC, KC)
            term = product(rows[i, h, :, :, :, cols].reshape(FLAT, KC), h, cols)
            dst[...] = term if (h, c) == (0, 0) else dst[...] + term

    def by_gate_up(left, h, cols):
        return jnp.dot(left, wgu[h, cols, :], preferred_element_type=F32)

    def by_down(left, h, cols):
        return contract_last(left, wd[h, :, cols])

    def gate_up(i, h):
        accumulate(acc.at[0 if i == BWD else 1], i, h, by_gate_up)

    def grad_hidden(h):
        accumulate(gh, GRAD, h, by_down)

    GATE, UP = pl.ds(0, FFD), pl.ds(FFD, FFD)

    def act_rowg():
        gate = acc[0, :, GATE]
        sigma = jax.nn.sigmoid(gate)
        grad = gh[...]
        act[0, :, GATE] = (
            grad * acc[0, :, UP] * sigma * (1.0 + gate * (1.0 - sigma))
        ).astype(BF16)
        act[0, :, UP] = (grad * (gate * sigma)).astype(BF16)

    def act_out():
        gate = acc[1, :, GATE]
        act[1, :, GATE] = (gate * jax.nn.sigmoid(gate) * acc[1, :, UP]).astype(BF16)

    NC = C // 3 if C % 384 == 0 else C

    def partial(j, h, c):
        for n in range(C // NC):
            if j == OUT:
                term = jnp.dot(
                    act[1, :, GATE],
                    wd[h, :, pl.ds(c * C + n * NC, NC)],
                    preferred_element_type=F32,
                )
            else:
                term = contract_last(act[0], wgu[h, pl.ds(c * C + n * NC, NC), :])
            term = term.astype(BF16).reshape(SIDE, SIDE, PAIR, NC)
            cols = pl.ds(n * NC, NC)
            if h == 0:
                part[j, 0, c, :, :, :, cols] = term
            else:
                for line in range(SIDE):
                    part[j, 1, c, line, :, :, cols] = term[:, line]

    def chip_sum(j, line, c):
        return part[j, 0, c, line].astype(F32) + sib_part[j, c, line].astype(F32)

    def send_b(j, m, line, c, plus=None):
        value = chip_sum(j, line, c)
        if plus is not None:
            value = value + b_in[j, plus].astype(F32)
        b_out[j, m] = value.astype(BF16)
        go(r[j]["b", m])

    def line_sum(j, c):
        one, two = 2 + c, 4 + c
        arrive(r[j]["b", one])
        arrive(r[j]["b", two])
        total = chip_sum(j, 0, c) + b_in[j, one].astype(F32) + b_in[j, two].astype(F32)
        a_out[j, c] = total[1:].astype(BF16)
        w_sum[j, c] = total[0]
        for m in range(3):
            go(r[j]["a", c, m])

    def block_sum(j, c):
        total = w_sum[j, c]
        for m in range(3):
            arrive(r[j]["a", c, m])
            total = total + a_in[j, c, m].astype(F32)
        final[j, :, pl.ds(pl.multiple_of(core * H + c * C, C), C)] = total.astype(BF16)
        go(r[j]["end", c])

    def half_lanes(h, k):
        start = (core if h == 0 else 1 - core) * H
        return pl.ds(pl.multiple_of(start + k * LANES, LANES), LANES)

    def project():
        inverse = inverse_v[:, pl.ds(0, 1)]
        total = jnp.zeros((PAIR, 1), F32)
        for k in range(D // LANES):
            adjusted = final[ROWG, :, lanes(k)].astype(F32) * gain_v[:, lanes(k)]
            total = total + jnp.sum(adjusted * picked[0, :, lanes(k)], axis=1, keepdims=True)
        factor = (inverse * inverse * inverse) * (total * (1.0 / D))
        for k in range(D // LANES):
            adjusted = final[ROWG, :, lanes(k)].astype(F32) * gain_v[:, lanes(k)]
            change = adjusted * inverse - picked[0, :, lanes(k)] * factor
            high = change.astype(BF16)
            changes[0, :, lanes(k)] = high
            changes[1, :, lanes(k)] = (change - high.astype(F32)).astype(BF16)

    def finish_grad():
        pick = token_pick(1)
        for k in range(D // LANES):
            cols = lanes(k)
            out_grad[0, :, cols] = (
                grad_v[:, cols].astype(F32)
                + jnp.dot(pick, changes[0, :, cols], preferred_element_type=F32)
                + jnp.dot(pick, changes[1, :, cols], preferred_element_type=F32)
            ).astype(BF16)

    def finish_fwd(h):
        pick = token_pick(0)
        scale = column(weight_v[pl.ds(0, 1), :])

        for k in range(H // LANES):
            cols = half_lanes(h, k)
            spread = jnp.dot(pick, final[OUT, :, cols], preferred_element_type=F32)
            out_fwd[0, :, cols] = (fwd_v[:, cols].astype(F32) + scale * spread).astype(BF16)

    def tile_of(i):
        if i == GRAD:

            @pl.when(section != n_pipe - 1)
            def _():
                send_grad.wait_recv()

            @pl.when(section == n_pipe - 1)
            def _():
                load_loss.wait()

            grad_tile(GRAD, grad_v, 1)
        elif i == FWD:

            @pl.when(section != 0)
            def _():
                send_fwd.wait_recv()

            @pl.when(section == 0)
            def _():
                load_fresh.wait()

            normed_tile(FWD, fwd_v, 0)
        go(g[i]["tile"])

    def own(i):
        arrive(g[i]["tile"])
        rows[i, 0, 0, 0] = tile[i, :, own_cols] + sib_tile[i]
        for name in ("au", "ad", "ax"):
            go(g[i][name])

    def own_b(i):
        go(g[i]["bu", 0])
        go(g[i]["bd", 0])

    def pair(i):
        arrive(g[i]["au"])
        arrive(g[i]["ad"])
        go(g[i]["bu", 1])
        go(g[i]["bd", 1])

    def opposite(i):
        arrive(g[i]["ax"])
        go(g[i]["bu", 2])
        go(g[i]["bd", 2])
        go(g[i]["s", 0])

    def forward_up(i, k):
        arrive(g[i]["bu", k])
        go(g[i]["bu2", k])
        if k == 2:
            go(g[i]["s", 2])

    def forward_dn(i, k):
        arrive(g[i]["bd", k])
        go(g[i]["bd2", k])
        if k == 2:
            go(g[i]["s", 1])

    def last_pair(i):
        for k in range(2):
            arrive(g[i]["bu2", k])
            arrive(g[i]["bd2", k])
        go(g[i]["s", 3])

    def last(i):
        arrive(g[i]["bu2", 2])
        arrive(g[i]["bd2", 2])
        go(g[i]["s", 4])

    def handed(i):
        for line in range(5):
            arrive(g[i]["s", line])

    def weights_gu():
        for copy in load_gu:
            copy.wait()

    def weights_d():
        for copy in load_d:
            copy.wait()

    def p1(j, c):
        partial(j, 1, c)
        for k in range(3):
            go(r[j]["sib", k, c])

    def p0(j, c):
        partial(j, 0, c)

    def m0(j):
        arrive(r[j]["sib", 0, 0])
        send_b(j, 0, 3, 0)

    def m1(j):
        arrive(r[j]["sib", 0, 1])
        send_b(j, 1, 3, 1)

    def m2(j):
        arrive(r[j]["sib", 1, 0])
        send_b(j, 2, 2, 0)

    def m3(j):
        arrive(r[j]["sib", 1, 1])
        send_b(j, 3, 1, 1)

    def m4(j):
        arrive(r[j]["b", 0])
        send_b(j, 4, 1, 0, plus=0)

    def m5(j):
        arrive(r[j]["b", 1])
        send_b(j, 5, 2, 1, plus=1)

    def w(j, c):
        arrive(r[j]["sib", 2, c])
        line_sum(j, c)

    def ended(j):
        for c in range(2):
            arrive(r[j]["end", c])

    tasks = dict(
        tile=tile_of,
        own=own,
        own_b=own_b,
        pair=pair,
        opposite=opposite,
        fu=forward_up,
        fd=forward_dn,
        last_pair=last_pair,
        last=last,
        handed=handed,
        gu=gate_up,
        gh=grad_hidden,
        act_rowg=act_rowg,
        act_out=act_out,
        p1=p1,
        p0=p0,
        m0=m0,
        m1=m1,
        m2=m2,
        m3=m3,
        m4=m4,
        m5=m5,
        w=w,
        x=block_sum,
        ended=ended,
        project=project,
        finish_grad=finish_grad,
        finish_fwd=finish_fwd,
        weights_gu=weights_gu,
        weights_d=weights_d,
    )

    inverse = normed_tile(BWD, saved_v, 1)
    inverse_v[...] = jnp.broadcast_to(inverse, inverse_v.shape)
    pl.semaphore_wait(barrier, 8)

    send_fwd = pltpu.make_async_remote_copy(
        src_ref=handed_fwd.at[0],
        dst_ref=fwd_v,
        send_sem=z_send.at[0],
        recv_sem=z_recv.at[0],
        device_id={"pipe": Z_UP, "tensor": t},
        device_id_type=pl.DeviceIdType.MESH,
    )
    send_grad = pltpu.make_async_remote_copy(
        src_ref=handed_grads.at[0],
        dst_ref=grad_v,
        send_sem=z_send.at[1],
        recv_sem=z_recv.at[1],
        device_id={"pipe": Z_DN, "tensor": t},
        device_id_type=pl.DeviceIdType.MESH,
    )

    @pl.when(section != n_pipe - 1)
    def _():
        send_fwd.start()

    @pl.when(section != 0)
    def _():
        send_grad.start()

    @pl.when(section == 0)
    def _():
        load_fresh.start()

    @pl.when(section == n_pipe - 1)
    def _():
        load_loss.start()

    go(g[BWD]["tile"])
    for copy in load_gu + load_d:
        copy.start()
    for name, *at_ in ORDER:
        tasks[name](*at_)

    for copy in sent:
        copy.wait_send()

    @pl.when(section != n_pipe - 1)
    def _():
        send_fwd.wait_send()

    @pl.when(section != 0)
    def _():
        send_grad.wait_send()


def place(fwd_in, grad_in, fwd_out, grad_out, sem):
    copies = [
        pltpu.make_async_copy(fwd_in, fwd_out, sem.at[0]),
        pltpu.make_async_copy(grad_in, grad_out, sem.at[1]),
    ]
    for copy in copies:
        copy.start()
    for copy in copies:
        copy.wait()


def on_device(
    n_pipe,
    fresh_batch,
    handed_forward,
    saved_inputs,
    handed_grads,
    loss_grad,
    norm_gain,
    route_slot,
    route_weight,
    w_gate,
    w_up,
    w_down,
):
    TOKD, D = fresh_batch.shape
    FFD = w_down.shape[1]
    H, C = D // 2, D // 4
    FLAT = SIDE * SIDE * PAIR
    anywhere = pl.BlockSpec(memory_space=pl.ANY)
    vmem = pltpu.VMEM
    dma = pltpu.SemaphoreType.DMA
    shape = jax.ShapeDtypeStruct((1, TOKD, D), BF16)
    inside = vmem((1, TOKD, D), BF16)
    in_vmem = pl.BlockSpec(memory_space=vmem)
    results = pl.pallas_call(
        functools.partial(kernel, n_pipe),
        out_shape=(inside, inside),
        in_specs=[anywhere] * 11,
        out_specs=(in_vmem, in_vmem),
        scratch_shapes=[
            vmem((TOKD, D), BF16),
            vmem((TOKD, D), BF16),
            vmem((TOKD, D), BF16),
            vmem((1, D), F32),
            vmem((2, TOKD), jnp.int32),
            vmem((2, TOKD), F32),
            vmem((2, H, 2 * FFD), BF16),
            vmem((2, FFD, H), BF16),
            vmem((2, PAIR, D), F32),
            vmem((3, PAIR, D), BF16),
            vmem((3, PAIR, H), BF16),
            vmem((3, 2, SIDE, SIDE, PAIR, H), BF16),
            vmem((2, FLAT, 2 * FFD), F32),
            vmem((FLAT, FFD), F32),
            vmem((2, FLAT, 2 * FFD), BF16),
            vmem((2, 2, 2, SIDE, SIDE, PAIR, C), BF16),
            vmem((2, 2, SIDE, SIDE, PAIR, C), BF16),
            vmem((2, 6, SIDE, PAIR, C), BF16),
            vmem((2, 6, SIDE, PAIR, C), BF16),
            vmem((2, 2, PAIR, C), F32),
            vmem((2, 2, 3, PAIR, C), BF16),
            vmem((2, 2, 3, PAIR, C), BF16),
            vmem((2, PAIR, D), BF16),
            vmem((PAIR, 128), F32),
            vmem((2, PAIR, D), BF16),
            dma((12,)),
            dma((2,)),
            dma((2,)),
            dma((3, 21)),
            dma((3, 21)),
            dma((2, 20)),
            dma((2, 20)),
        ],
        compiler_params=pltpu.CompilerParams(
            collective_id=0, has_side_effects=True, vmem_limit_bytes=56 * 2**20
        ),
    )(
        fresh_batch,
        handed_forward,
        saved_inputs,
        handed_grads,
        loss_grad,
        norm_gain,
        route_slot,
        route_weight,
        w_gate,
        w_up,
        w_down,
    )
    return pl.pallas_call(
        place,
        out_shape=(shape, shape),
        in_specs=[in_vmem] * 2,
        out_specs=(anywhere, anywhere),
        scratch_shapes=[dma((2,))],
        compiler_params=pltpu.CompilerParams(vmem_limit_bytes=8 * 2**20),
    )(*results)


def solution(mesh):
    placed = (
        P("tensor", None),
        P("pipe", "tensor", None),
        P("pipe", "tensor", None),
        P("pipe", "tensor", None),
        P("tensor", None),
        P("pipe", None),
        P("pipe", None, "tensor"),
        P("pipe", None, "tensor"),
        P("pipe", None, "tensor"),
        P("pipe", None, "tensor"),
        P("pipe", "tensor", None),
    )
    return jax.shard_map(
        functools.partial(on_device, mesh.shape["pipe"]),
        mesh=mesh,
        in_specs=placed,
        out_specs=(P("pipe", "tensor", None), P("pipe", "tensor", None)),
        check_vma=False,
    )
```

time: 327 us -> 70.7 us (0.22)
  waiting for transfers between devices: 257 us -> 0 us
  Pallas kernels: 0 us -> 69.9 us
  matrix products: 41.4 us -> 0 us
  between operations: 13.9 us -> 0.64 us
  starting transfers between devices: 6.11 us -> 0 us
  other arithmetic: 5.7 us -> 0 us
    reduce_scatter x2 -> x0, waiting for transfers between devices: 156 us -> none  [reduce_rows(): lax.psum_scatter(jnp.concatenate([make(start, LCAP * lax.axis_size('tenso...]
    all_gather x2 -> x0, waiting for transfers between devices: 86.5 us -> none  [expand(): piece = lax.all_gather(stacked, 'tensor', axis=0, tiled=True)]
    pallas_call x0 -> x2, Pallas kernels: none -> 69.9 us  [the longest x1 69 us: on_device(): pl.pallas_call(functools.partial(kernel, n_pipe), out_shape=(inside, insi...]
    dot_general x11 -> x0, matrix products: 41.4 us -> none  [the longest x3 18.3 us: contract_last(): lax.dot_general(left, right, (((1,), (1,)), ((), ())), preferred_element_...]
    ppermute x2 -> x0, waiting for transfers between devices: 14.1 us -> none  [passed_along(): return lax.ppermute(value, axis, pairs)]
    ppermute x2 -> x0, starting transfers between devices: 5.95 us -> none  [passed_along(): return lax.ppermute(value, axis, pairs)]
  transfers between devices with their start and end apart: 6 -> 0, of which waited for: 6 -> 0; matrix products, arithmetic and copies ran while one was open for 13% -> 0% of each run, Pallas kernels for 0% -> 0%
where the time goes in v2:
time: 70.7 us; the launch traced here: 70.6 us
  Pallas kernels  69.9 us (99%)
    pallas_call x1, Pallas kernels, on_device(): pl.pallas_call(functools.partial(kernel, n_pipe), out_shape=(inside, insi...  69 us

profile of v2, /device:TPU:1, one launch (start us, length us, event | category | flops | bytes accessed | tf_op | source)
XLA Modules:
  0.0 70.6 jit_solution(8250962499315430492)
XLA Ops:
  0.6 69.0 %shard_map.122 = (bf16[1,32,6144]{2,1,0:T(8,128)(2,1)S(1)}, bf16[1,32,6144]{2,1,0:T(8,128)(2,1)S(1)}) custom-call(bf16[32,6144]{1,0:T(8,128)(2,1)} %fresh.1, bf16[1,32,6144]{2,1,0:T(8,128)(2,1)} %handed_fwd.1, bf16[1,32,6144]{2,1,0:T(8,128)(2,1)} %saved.1, bf16[1,32,6144]{2,1,0:T(8,128)(2,1)} %handed_grads.1, bf16[32,6144]{1,0:T(8,128)(2,1)} %loss_grad.1, ...), custom_call_target="tpu_custom_call" | custom-call | tf_op jit(solution)/shard_map/pallas_call | solution.py:656
  69.7 0.9 %shard_map.123 = (bf16[1,32,6144]{2,1,0:T(8,128)(2,1)}, bf16[1,32,6144]{2,1,0:T(8,128)(2,1)}) custom-call(bf16[1,32,6144]{2,1,0:T(8,128)(2,1)S(1)} %get-tuple-element.4.fwd_in, bf16[1,32,6144]{2,1,0:T(8,128)(2,1)S(1)} %get-tuple-element.5.grad_in), custom_call_target="tpu_custom_call" | custom-call | tf_op jit(solution)/shard_map/pallas_call | solution.py:711

commit v3 on v2

--- a/solution.py
+++ b/solution.py
@@ -14,26 +14,31 @@
 F32 = jnp.float32
 BF16 = jnp.bfloat16
 BWD, GRAD, FWD = 0, 1, 2
+FWD_WAY, GRAD_WAY = 0, 1
 ROWG, OUT = 0, 1
 
 
 def contract_last(left, right):
     return lax.dot_general(left, right, (((1,), (1,)), ((), ())), preferred_element_type=F32)
+HOPS_G = (False, True, True)
+HOPS_R = (True, False)
 ORDER = (
-    ("own", 0), ("weights_gu",), ("own_b", 0), ("pair", 0), ("fd", 0, 0), ("opposite", 0),
-    ("fu", 0, 1), ("tile", 1), ("fd", 0, 1), ("fu", 0, 0), ("fd", 0, 2), ("own", 1),
-    ("fu", 0, 2), ("tile", 2), ("own_b", 1), ("last_pair", 0), ("own", 2), ("last", 0),
-    ("pair", 1), ("opposite", 1), ("gu", 0, 0), ("fd", 1, 0), ("fu", 1, 0), ("weights_d",),
-    ("own_b", 2), ("fd", 1, 1), ("fu", 1, 1), ("fd", 1, 2), ("fu", 1, 2), ("pair", 2),
-    ("handed", 0), ("opposite", 2), ("fu", 2, 0), ("fd", 2, 0), ("gu", 0, 1), ("last_pair", 1),
-    ("last", 1), ("gh", 0), ("handed", 1), ("gh", 1), ("act_rowg",), ("fu", 2, 1), ("fd", 2, 1),
-    ("p0", 0, 0), ("fd", 2, 2), ("fu", 2, 2), ("p1", 0, 1), ("p1", 0, 0), ("p0", 0, 1),
-    ("m1", 0), ("last_pair", 2), ("m3", 0), ("last", 2), ("gu", 2, 0), ("m0", 0), ("m2", 0),
-    ("handed", 2), ("gu", 2, 1), ("act_out",), ("p1", 1, 0), ("p1", 1, 1), ("p0", 1, 0),
-    ("m0", 1), ("m5", 0), ("p0", 1, 1), ("m3", 1), ("m1", 1), ("m2", 1), ("m4", 0), ("m4", 1),
-    ("m5", 1), ("w", 0, 0), ("w", 0, 1), ("w", 1, 0), ("w", 1, 1), ("x", 0, 0), ("x", 0, 1),
-    ("x", 1, 0), ("ended", 0), ("project",), ("x", 1, 1), ("finish_fwd", 0), ("finish_grad",),
-    ("ended", 1), ("finish_fwd", 1),
+    ("own", 0), ("pack", 1), ("pack", 2), ("own_b", 0), ("pair", 0), ("opposite", 0),
+    ("weights_d",), ("tile", 1), ("fd", 0, 0), ("fu", 0, 0), ("own", 1), ("fd", 0, 1),
+    ("fu", 0, 1), ("tile", 2), ("own_b", 1), ("own", 2), ("fa", 1), ("weights_gu",),
+    ("pair", 1), ("last_pair", 0), ("fu", 0, 2), ("fa", 2), ("fd", 0, 2), ("opposite", 1),
+    ("own_b", 2), ("fd", 1, 0), ("fu", 1, 0), ("fu", 1, 1), ("last", 0), ("fd", 1, 1),
+    ("gu", 0, 0), ("fu", 1, 2), ("fd", 1, 2), ("pair", 2), ("opposite", 2), ("handed", 0),
+    ("gu", 0, 1), ("fd", 2, 0), ("last_pair", 1), ("last", 1), ("fu", 2, 0), ("gh", 0),
+    ("handed", 1), ("gh", 1), ("relay_all",), ("act_rowg",), ("p1", 0, 1), ("fd", 2, 1),
+    ("fu", 2, 1), ("p1", 0, 0), ("fd", 2, 2), ("fu", 2, 2), ("p0", 0, 1), ("m1", 0),
+    ("p0", 0, 0), ("m0", 0), ("m3", 0), ("m2", 0), ("last_pair", 2), ("last", 2), ("gu", 2, 0),
+    ("handed", 2), ("gu", 2, 1), ("act_out",), ("m5", 0), ("p1", 1, 1), ("m4", 0), ("p0", 1, 1),
+    ("p1", 1, 0), ("m1", 1), ("p0", 1, 0), ("m0", 1), ("m3", 1), ("m2", 1), ("w", 0, 1),
+    ("m5", 1), ("w", 0, 0), ("m4", 1), ("v", 0, 0), ("v", 0, 1), ("w", 1, 1), ("w", 1, 0),
+    ("x", 0, 0), ("x", 0, 1), ("ended", 0), ("project",), ("relayed", 1), ("finish_grad",),
+    ("x", 1, 1), ("x", 1, 0), ("relayed", 2), ("finish_fwd", 0), ("ended", 1),
+    ("finish_fwd", 1),
 )
 
 
@@ -58,6 +63,10 @@
     gain_v,
     slot_v,
     weight_v,
+    source_v,
+    slots_v,
+    packed_out,
+    packed_in,
     wgu,
     wd,
     picked,
@@ -136,7 +145,11 @@
     ]
     load_fresh = local(fresh, fwd_v, 10)
     load_loss = local(loss_grad, grad_v, 11)
-    for copy in first:
+    load_sources = [
+        local(handed_fwd.at[0], source_v.at[FWD_WAY], 12),
+        local(handed_grads.at[0], source_v.at[GRAD_WAY], 13),
+    ]
+    for copy in first + load_sources:
         copy.start()
 
     barrier = pltpu.get_barrier_semaphore()
@@ -197,12 +210,41 @@
     def lanes(k):
         return pl.ds(k * LANES, LANES)
 
-    def normed_tile(i, source, micro):
-        pick = row_pick(micro).astype(BF16)
+    def pack(source, slots):
+        places = lax.broadcasted_iota(jnp.int32, (PAIR, TOKD), 0)
+        slots = jnp.broadcast_to(slots, (PAIR, TOKD))
+        low = jnp.where((places == slots) & (places < LCAP), 1.0, 0.0).astype(BF16)
+        high = jnp.where((places - LCAP == slots) & (slots < LCAP), 1.0, 0.0).astype(BF16)
+        parts = []
+        for k in range(H // LANES):
+            parts.append(
+                jnp.dot(low, source[:, lanes(k)], preferred_element_type=F32)
+                + jnp.dot(high, source[:, lanes(k + H // LANES)], preferred_element_type=F32)
+            )
+        return parts
+
+    def store_pack(dst, parts):
+        for k, value in enumerate(parts):
+            dst[:, lanes(k)] = value.astype(BF16)
+
+    def unpacked(way, k):
+        half, k = k // (H // LANES), k % (H // LANES)
+        places = lax.broadcasted_iota(jnp.int32, (PAIR, PAIR), 0) - core * LCAP
+        origin = lax.broadcasted_iota(jnp.int32, (PAIR, PAIR), 1) - half * LCAP
+        pick = jnp.where((places == origin) & (places >= 0) & (places < LCAP), 1.0, 0.0)
+        return jnp.dot(
+            pick.astype(BF16), packed_in[way, :, lanes(k)], preferred_element_type=F32
+        )
+
+    def normed_tile(i):
+        pick = row_pick(1).astype(BF16)
         place = 0 if i == BWD else 1
         total = jnp.zeros((PAIR, 1), F32)
         for k in range(D // LANES):
-            z = jnp.dot(pick, source[:, lanes(k)], preferred_element_type=F32)
+            if i == BWD:
+                z = jnp.dot(pick, saved_v[:, lanes(k)], preferred_element_type=F32)
+            else:
+                z = unpacked(FWD_WAY, k)
             picked[place, :, lanes(k)] = z
             total = total + jnp.sum(z * z, axis=1, keepdims=True)
         inverse = lax.rsqrt(total * (1.0 / D) + EPS)
@@ -212,24 +254,22 @@
             ).astype(BF16)
         return inverse
 
-    def grad_tile(i, source, micro):
-        pick_f = row_pick(micro)
-        pick = pick_f.astype(BF16)
+    def grad_tile():
+        pick = row_pick(1)
         weights = jnp.sum(
-            pick_f * jnp.broadcast_to(weight_v[pl.ds(micro, 1), :], (PAIR, TOKD)),
+            pick * jnp.broadcast_to(weight_v[pl.ds(1, 1), :], (PAIR, TOKD)),
             axis=1,
             keepdims=True,
         )
-
         for k in range(D // LANES):
-            g = jnp.dot(pick, source[:, lanes(k)], preferred_element_type=F32)
-            tile[i, :, lanes(k)] = (weights * g).astype(BF16)
+            g = unpacked(GRAD_WAY, k)
+            tile[GRAD, :, lanes(k)] = (weights * g).astype(BF16)
 
     C0, C1 = pl.ds(0, C), pl.ds(C, C)
     PAIR_OF = pl.ds(1, 2)
 
     def gather(i):
-        count = iter(range(21))
+        count = iter(range(22))
 
         def send(src, dst, tensor):
             m = next(count)
@@ -240,8 +280,12 @@
             "tile": send(tile.at[i, :, oth], sib_tile.at[i], SIB),
             "au": send(mine.at[0, 0], mine.at[0, 2], A_UP),
             "ad": send(mine.at[0, 0], mine.at[0, 1], A_DN),
-            "ax": send(mine.at[0, 0], mine.at[0, 3], A_OP),
         }
+        if HOPS_G[i]:
+            copies["au2"] = send(mine.at[0, 2, :, C0], mine.at[0, 3, :, C0], A_UP)
+            copies["ad2"] = send(mine.at[0, 1, :, C1], mine.at[0, 3, :, C1], A_DN)
+        else:
+            copies["ax"] = send(mine.at[0, 0], mine.at[0, 3], A_OP)
         for k, group in enumerate((pl.ds(0, 1), PAIR_OF, pl.ds(3, 1))):
             copies["bu", k] = send(mine.at[0, group], mine.at[2, group], B_UP)
             copies["bd", k] = send(mine.at[0, group], mine.at[1, group], B_DN)
@@ -276,7 +320,8 @@
         for m, tensor in enumerate((B_UP, B_DN, B_DN, B_UP, B_UP, B_DN)):
             copies["b", m] = send(b_out.at[j, m], b_in.at[j, m], tensor)
         for c in range(2):
-            for m, tensor in enumerate((A_UP, A_DN, A_OP)):
+            far = (A_UP, A_DN)[c] if HOPS_R[j] else A_OP
+            for m, tensor in enumerate((A_UP, A_DN, far)):
                 copies["a", c, m] = send(a_out.at[j, c, m], a_in.at[j, c, m], tensor)
             cols = pl.ds(pl.multiple_of(core * H + c * C, C), C)
             copies["end", c] = send(final.at[j, :, cols], final.at[j, :, cols], SIB)
@@ -358,14 +403,26 @@
         arrive(r[j]["b", one])
         arrive(r[j]["b", two])
         total = chip_sum(j, 0, c) + b_in[j, one].astype(F32) + b_in[j, two].astype(F32)
-        a_out[j, c] = total[1:].astype(BF16)
-        w_sum[j, c] = total[0]
-        for m in range(3):
-            go(r[j]["a", c, m])
+        w_sum[j, c, 0] = total[0]
+        if HOPS_R[j]:
+            w_sum[j, c, 1] = total[1 + c]
+            a_out[j, c, 2] = total[3].astype(BF16)
+            a_out[j, c, 1 - c] = total[2 - c].astype(BF16)
+            go(r[j]["a", c, 2])
+            go(r[j]["a", c, 1 - c])
+        else:
+            a_out[j, c] = total[1:].astype(BF16)
+            for m in range(3):
+                go(r[j]["a", c, m])
+
+    def hop_r(j, c):
+        arrive(r[j]["a", c, 2])
+        a_out[j, c, c] = (w_sum[j, c, 1] + a_in[j, c, 2].astype(F32)).astype(BF16)
+        go(r[j]["a", c, c])
 
     def block_sum(j, c):
-        total = w_sum[j, c]
-        for m in range(3):
+        total = w_sum[j, c, 0]
+        for m in range(2) if HOPS_R[j] else range(3):
             arrive(r[j]["a", c, m])
             total = total + a_in[j, c, m].astype(F32)
         final[j, :, pl.ds(pl.multiple_of(core * H + c * C, C), C)] = total.astype(BF16)
@@ -408,49 +465,104 @@
             spread = jnp.dot(pick, final[OUT, :, cols], preferred_element_type=F32)
             out_fwd[0, :, cols] = (fwd_v[:, cols].astype(F32) + scale * spread).astype(BF16)
 
+    def pack_of(i):
+        if i == GRAD:
+            load_sources[GRAD_WAY].wait()
+            slots_up.wait_recv()
+            store_pack(
+                packed_out.at[GRAD_WAY],
+                pack(source_v.at[GRAD_WAY], slots_v[GRAD_WAY, pl.ds(1, 1), :]),
+            )
+
+            @pl.when(section != 0)
+            def _():
+                rows_dn.start()
+        else:
+            load_sources[FWD_WAY].wait()
+            slots_dn.wait_recv()
+            store_pack(
+                packed_out.at[FWD_WAY],
+                pack(source_v.at[FWD_WAY], slots_v[FWD_WAY, pl.ds(0, 1), :]),
+            )
+
+            @pl.when(section != n_pipe - 1)
+            def _():
+                rows_up.start()
+
+    def relay_all():
+        @pl.when(section != 0)
+        def _():
+            send_grad.start()
+
+        @pl.when(section != n_pipe - 1)
+        def _():
+            send_fwd.start()
+
     def tile_of(i):
+        if i == GRAD:
+
+            @pl.when(section != n_pipe - 1)
+            def _():
+                rows_dn.wait_recv()
+
+            @pl.when(section == n_pipe - 1)
+            def _():
+                load_loss.wait()
+                store_pack(packed_in.at[GRAD_WAY], pack(grad_v, slot_v[pl.ds(1, 1), :]))
+
+            grad_tile()
+        elif i == FWD:
+
+            @pl.when(section != 0)
+            def _():
+                rows_up.wait_recv()
+
+            @pl.when(section == 0)
+            def _():
+                load_fresh.wait()
+                store_pack(packed_in.at[FWD_WAY], pack(fwd_v, slot_v[pl.ds(0, 1), :]))
+
+            normed_tile(FWD)
+        go(g[i]["tile"])
+
+    def relayed(i):
         if i == GRAD:
 
             @pl.when(section != n_pipe - 1)
             def _():
                 send_grad.wait_recv()
-
-            @pl.when(section == n_pipe - 1)
-            def _():
-                load_loss.wait()
-
-            grad_tile(GRAD, grad_v, 1)
-        elif i == FWD:
+        else:
 
             @pl.when(section != 0)
             def _():
                 send_fwd.wait_recv()
 
-            @pl.when(section == 0)
-            def _():
-                load_fresh.wait()
-
-            normed_tile(FWD, fwd_v, 0)
-        go(g[i]["tile"])
-
     def own(i):
         arrive(g[i]["tile"])
         rows[i, 0, 0, 0] = tile[i, :, own_cols] + sib_tile[i]
-        for name in ("au", "ad", "ax"):
+        for name in ("au", "ad") if HOPS_G[i] else ("au", "ad", "ax"):
             go(g[i][name])
 
     def own_b(i):
         go(g[i]["bu", 0])
         go(g[i]["bd", 0])
 
-    def pair(i):
+    def hop_a(i):
         arrive(g[i]["au"])
         arrive(g[i]["ad"])
+        go(g[i]["au2"])
+        go(g[i]["ad2"])
+
+    def pair(i):
+        if not HOPS_G[i]:
+            arrive(g[i]["au"])
+            arrive(g[i]["ad"])
         go(g[i]["bu", 1])
         go(g[i]["bd", 1])
 
     def opposite(i):
-        arrive(g[i]["ax"])
+        for name in ("au2", "ad2") if HOPS_G[i] else ("ax",):
+            arrive(g[i][name])
         go(g[i]["bu", 2])
         go(g[i]["bd", 2])
         go(g[i]["s", 0])
@@ -531,9 +643,13 @@
             arrive(r[j]["end", c])
 
     tasks = dict(
+        pack=pack_of,
         tile=tile_of,
+        relayed=relayed,
+        relay_all=relay_all,
         own=own,
         own_b=own_b,
+        fa=hop_a,
         pair=pair,
         opposite=opposite,
         fu=forward_up,
@@ -554,6 +670,7 @@
         m4=m4,
         m5=m5,
         w=w,
+        v=hop_r,
         x=block_sum,
         ended=ended,
         project=project,
@@ -563,7 +680,7 @@
         weights_d=weights_d,
     )
 
-    inverse = normed_tile(BWD, saved_v, 1)
+    inverse = normed_tile(BWD)
     inverse_v[...] = jnp.broadcast_to(inverse, inverse_v.shape)
     pl.semaphore_wait(barrier, 8)
 
@@ -584,13 +701,40 @@
         device_id_type=pl.DeviceIdType.MESH,
     )
 
-    @pl.when(section != n_pipe - 1)
-    def _():
-        send_fwd.start()
-
-    @pl.when(section != 0)
-    def _():
-        send_grad.start()
+    slots_dn = pltpu.make_async_remote_copy(
+        src_ref=slot.at[0],
+        dst_ref=slots_v.at[FWD_WAY],
+        send_sem=z_send.at[2],
+        recv_sem=z_recv.at[2],
+        device_id={"pipe": Z_DN, "tensor": t},
+        device_id_type=pl.DeviceIdType.MESH,
+    )
+    slots_up = pltpu.make_async_remote_copy(
+        src_ref=slot.at[0],
+        dst_ref=slots_v.at[GRAD_WAY],
+        send_sem=z_send.at[3],
+        recv_sem=z_recv.at[3],
+        device_id={"pipe": Z_UP, "tensor": t},
+        device_id_type=pl.DeviceIdType.MESH,
+    )
+    slots_dn.start()
+    slots_up.start()
+    rows_up = pltpu.make_async_remote_copy(
+        src_ref=packed_out.at[FWD_WAY],
+        dst_ref=packed_in.at[FWD_WAY],
+        send_sem=z_send.at[4],
+        recv_sem=z_recv.at[4],
+        device_id={"pipe": Z_UP, "tensor": t},
+        device_id_type=pl.DeviceIdType.MESH,
+    )
+    rows_dn = pltpu.make_async_remote_copy(
+        src_ref=packed_out.at[GRAD_WAY],
+        dst_ref=packed_in.at[GRAD_WAY],
+        send_sem=z_send.at[5],
+        recv_sem=z_recv.at[5],
+        device_id={"pipe": Z_DN, "tensor": t},
+        device_id_type=pl.DeviceIdType.MESH,
+    )
 
     @pl.when(section == 0)
     def _():
@@ -609,12 +753,17 @@
     for copy in sent:
         copy.wait_send()
 
+    slots_dn.wait_send()
+    slots_up.wait_send()
+
     @pl.when(section != n_pipe - 1)
     def _():
+        rows_up.wait_send()
         send_fwd.wait_send()
 
     @pl.when(section != 0)
     def _():
+        rows_dn.wait_send()
         send_grad.wait_send()
 
 
@@ -665,6 +814,10 @@
             vmem((1, D), F32),
             vmem((2, TOKD), jnp.int32),
             vmem((2, TOKD), F32),
+            vmem((2, TOKD, D), BF16),
+            vmem((2, 2, TOKD), jnp.int32),
+            vmem((2, PAIR, H), BF16),
+            vmem((2, PAIR, H), BF16),
             vmem((2, H, 2 * FFD), BF16),
             vmem((2, FFD, H), BF16),
             vmem((2, PAIR, D), F32),
@@ -678,17 +831,17 @@
             vmem((2, 2, SIDE, SIDE, PAIR, C), BF16),
             vmem((2, 6, SIDE, PAIR, C), BF16),
             vmem((2, 6, SIDE, PAIR, C), BF16),
-            vmem((2, 2, PAIR, C), F32),
+            vmem((2, 2, 2, PAIR, C), F32),
             vmem((2, 2, 3, PAIR, C), BF16),
             vmem((2, 2, 3, PAIR, C), BF16),
             vmem((2, PAIR, D), BF16),
             vmem((PAIR, 128), F32),
             vmem((2, PAIR, D), BF16),
-            dma((12,)),
-            dma((2,)),
-            dma((2,)),
-            dma((3, 21)),
-            dma((3, 21)),
+            dma((14,)),
+            dma((6,)),
+            dma((6,)),
+            dma((3, 22)),
+            dma((3, 22)),
             dma((2, 20)),
             dma((2, 20)),
         ],

time: 70.7 us -> 68.5 us (0.969)
  Pallas kernels: 69.9 us -> 67.7 us
    pallas_call x1, Pallas kernels: 69 us -> 66.8 us  [on_device(): pl.pallas_call(functools.partial(kernel, n_pipe), out_shape=(inside, insi...]
where the time goes in v3:
time: 68.5 us; the launch traced here: 68.4 us
  Pallas kernels  67.7 us (99%)
    pallas_call x1, Pallas kernels, on_device(): pl.pallas_call(functools.partial(kernel, n_pipe), out_shape=(inside, insi...  66.8 us

profile of v3, /device:TPU:1, one launch (start us, length us, event | category | flops | bytes accessed | tf_op | source)
XLA Modules:
  0.0 68.4 jit_solution(7851984896844125650)
XLA Ops:
  0.6 66.8 %shard_map.122 = (bf16[1,32,6144]{2,1,0:T(8,128)(2,1)S(1)}, bf16[1,32,6144]{2,1,0:T(8,128)(2,1)S(1)}) custom-call(bf16[32,6144]{1,0:T(8,128)(2,1)} %fresh.1, bf16[1,32,6144]{2,1,0:T(8,128)(2,1)} %handed_fwd.1, bf16[1,32,6144]{2,1,0:T(8,128)(2,1)} %saved.1, bf16[1,32,6144]{2,1,0:T(8,128)(2,1)} %handed_grads.1, bf16[32,6144]{1,0:T(8,128)(2,1)} %loss_grad.1, ...), custom_call_target="tpu_custom_call" | custom-call | tf_op jit(solution)/shard_map/pallas_call | solution.py:805
  67.5 0.9 %shard_map.123 = (bf16[1,32,6144]{2,1,0:T(8,128)(2,1)}, bf16[1,32,6144]{2,1,0:T(8,128)(2,1)}) custom-call(bf16[1,32,6144]{2,1,0:T(8,128)(2,1)S(1)} %get-tuple-element.4.fwd_in, bf16[1,32,6144]{2,1,0:T(8,128)(2,1)S(1)} %get-tuple-element.5.grad_in), custom_call_target="tpu_custom_call" | custom-call | tf_op jit(solution)/shard_map/pallas_call | solution.py:864

commit v4 on v3

--- a/solution.py
+++ b/solution.py
@@ -23,22 +23,101 @@
 HOPS_G = (False, True, True)
 HOPS_R = (True, False)
 ORDER = (
-    ("own", 0), ("pack", 1), ("pack", 2), ("own_b", 0), ("pair", 0), ("opposite", 0),
-    ("weights_d",), ("tile", 1), ("fd", 0, 0), ("fu", 0, 0), ("own", 1), ("fd", 0, 1),
-    ("fu", 0, 1), ("tile", 2), ("own_b", 1), ("own", 2), ("fa", 1), ("weights_gu",),
-    ("pair", 1), ("last_pair", 0), ("fu", 0, 2), ("fa", 2), ("fd", 0, 2), ("opposite", 1),
-    ("own_b", 2), ("fd", 1, 0), ("fu", 1, 0), ("fu", 1, 1), ("last", 0), ("fd", 1, 1),
-    ("gu", 0, 0), ("fu", 1, 2), ("fd", 1, 2), ("pair", 2), ("opposite", 2), ("handed", 0),
-    ("gu", 0, 1), ("fd", 2, 0), ("last_pair", 1), ("last", 1), ("fu", 2, 0), ("gh", 0),
-    ("handed", 1), ("gh", 1), ("relay_all",), ("act_rowg",), ("p1", 0, 1), ("fd", 2, 1),
-    ("fu", 2, 1), ("p1", 0, 0), ("fd", 2, 2), ("fu", 2, 2), ("p0", 0, 1), ("m1", 0),
-    ("p0", 0, 0), ("m0", 0), ("m3", 0), ("m2", 0), ("last_pair", 2), ("last", 2), ("gu", 2, 0),
-    ("handed", 2), ("gu", 2, 1), ("act_out",), ("m5", 0), ("p1", 1, 1), ("m4", 0), ("p0", 1, 1),
-    ("p1", 1, 0), ("m1", 1), ("p0", 1, 0), ("m0", 1), ("m3", 1), ("m2", 1), ("w", 0, 1),
-    ("m5", 1), ("w", 0, 0), ("m4", 1), ("v", 0, 0), ("v", 0, 1), ("w", 1, 1), ("w", 1, 0),
-    ("x", 0, 0), ("x", 0, 1), ("ended", 0), ("project",), ("relayed", 1), ("finish_grad",),
-    ("x", 1, 1), ("x", 1, 0), ("relayed", 2), ("finish_fwd", 0), ("ended", 1),
-    ("finish_fwd", 1),
+    ("own", 0),
+    ("pack", 1),
+    ("pack", 2),
+    ("own_b", 0),
+    ("pair", 0),
+    ("opposite", 0),
+    ("weights_d",),
+    ("tile", 1),
+    ("fd", 0, 0),
+    ("fu", 0, 0),
+    ("own", 1),
+    ("fd", 0, 1),
+    ("fu", 0, 1),
+    ("tile", 2),
+    ("own_b", 1),
+    ("own", 2),
+    ("fa", 1),
+    ("weights_gu",),
+    ("pair", 1),
+    ("last_pair", 0),
+    ("fu", 0, 2),
+    ("fa", 2),
+    ("fd", 0, 2),
+    ("opposite", 1),
+    ("own_b", 2),
+    ("fd", 1, 0),
+    ("fu", 1, 0),
+    ("fu", 1, 1),
+    ("last", 0),
+    ("fd", 1, 1),
+    ("gu", 0, 0),
+    ("fu", 1, 2),
+    ("fd", 1, 2),
+    ("pair", 2),
+    ("opposite", 2),
+    ("handed", 0),
+    ("gu", 0, 1),
+    ("fd", 2, 0),
+    ("last_pair", 1),
+    ("last", 1),
+    ("fu", 2, 0),
+    ("gh", 0),
+    ("handed", 1),
+    ("gh", 1),
+    ("relay_all",),
+    ("act_rowg",),
+    ("p1", 0, 1),
+    ("fd", 2, 1),
+    ("fu", 2, 1),
+    ("p1", 0, 0),
+    ("fd", 2, 2),
+    ("fu", 2, 2),
+    ("p0", 0, 1),
+    ("m1", 0),
+    ("p0", 0, 0),
+    ("m0", 0),
+    ("m3", 0),
+    ("m2", 0),
+    ("last_pair", 2),
+    ("last", 2),
+    ("gu", 2, 0),
+    ("handed", 2),
+    ("gu", 2, 1),
+    ("act_out",),
+    ("m5", 0),
+    ("p1", 1, 1),
+    ("m4", 0),
+    ("p0", 1, 1),
+    ("p1", 1, 0),
+    ("m1", 1),
+    ("p0", 1, 0),
+    ("m0", 1),
+    ("m3", 1),
+    ("m2", 1),
+    ("w", 0, 1),
+    ("m5", 1),
+    ("w", 0, 0),
+    ("m4", 1),
+    ("v", 0, 0),
+    ("v", 0, 1),
+    ("w", 1, 1),
+    ("w", 1, 0),
+    ("x", 0, 0),
+    ("x", 0, 1),
+    ("ended", 0),
+    ("project",),
+    ("relayed", 1),
+    ("finish_grad",),
+    ("relayed", 2),
+    ("x", 1, 1),
+    ("finish_fwd", 0, 1),
+    ("x", 1, 0),
+    ("finish_fwd", 1, 1),
+    ("finish_fwd", 0, 0),
+    ("finish_fwd", 1, 0),
 )
 
 
@@ -428,9 +507,9 @@
         final[j, :, pl.ds(pl.multiple_of(core * H + c * C, C), C)] = total.astype(BF16)
         go(r[j]["end", c])
 
-    def half_lanes(h, k):
+    def part_lanes(h, c, k):
         start = (core if h == 0 else 1 - core) * H
-        return pl.ds(pl.multiple_of(start + k * LANES, LANES), LANES)
+        return pl.ds(pl.multiple_of(start + c * C + k * NC, NC), NC)
 
     def project():
         inverse = inverse_v[:, pl.ds(0, 1)]
@@ -456,12 +535,14 @@
                 + jnp.dot(pick, changes[1, :, cols], preferred_element_type=F32)
             ).astype(BF16)
 
-    def finish_fwd(h):
+    def finish_fwd(h, c):
+        if h == 1:
+            arrive(r[OUT]["end", c])
         pick = token_pick(0)
         scale = column(weight_v[pl.ds(0, 1), :])
 
-        for k in range(H // LANES):
-            cols = half_lanes(h, k)
+        for k in range(C // NC):
+            cols = part_lanes(h, c, k)
             spread = jnp.dot(pick, final[OUT, :, cols], preferred_element_type=F32)
             out_fwd[0, :, cols] = (fwd_v[:, cols].astype(F32) + scale * spread).astype(BF16)
 

time: 68.5 us -> 68.5 us (level)
  no operation moved by 1% of the time
where the time goes in v4:
time: 68.5 us; the launch traced here: 68.4 us
  Pallas kernels  67.7 us (99%)
    pallas_call x1, Pallas kernels, on_device(): pl.pallas_call(functools.partial(kernel, n_pipe), out_shape=(inside, insi...  66.8 us

profile of v4, /device:TPU:1, one launch (start us, length us, event | category | flops | bytes accessed | tf_op | source)
XLA Modules:
  0.0 68.4 jit_solution(17977382197325765072)
XLA Ops:
  0.6 66.8 %shard_map.122 = (bf16[1,32,6144]{2,1,0:T(8,128)(2,1)S(1)}, bf16[1,32,6144]{2,1,0:T(8,128)(2,1)S(1)}) custom-call(bf16[32,6144]{1,0:T(8,128)(2,1)} %fresh.1, bf16[1,32,6144]{2,1,0:T(8,128)(2,1)} %handed_fwd.1, bf16[1,32,6144]{2,1,0:T(8,128)(2,1)} %saved.1, bf16[1,32,6144]{2,1,0:T(8,128)(2,1)} %handed_grads.1, bf16[32,6144]{1,0:T(8,128)(2,1)} %loss_grad.1, ...), custom_call_target="tpu_custom_call" | custom-call | tf_op jit(solution)/shard_map/pallas_call | solution.py:886
  67.5 0.9 %shard_map.123 = (bf16[1,32,6144]{2,1,0:T(8,128)(2,1)}, bf16[1,32,6144]{2,1,0:T(8,128)(2,1)}) custom-call(bf16[1,32,6144]{2,1,0:T(8,128)(2,1)S(1)} %get-tuple-element.4.fwd_in, bf16[1,32,6144]{2,1,0:T(8,128)(2,1)S(1)} %get-tuple-element.5.grad_in), custom_call_target="tpu_custom_call" | custom-call | tf_op jit(solution)/shard_map/pallas_call | solution.py:945
